TPU v7x, 32 devices: a whole 2x2x4 slice. The times are simulated.
32 devices in a mesh: tm: 8 (over z, x), head: 4 (over y, core).
Axes of the slice: x: 2, y: 2, z: 4, core: 2. Of those that a mesh axis runs over, the one named last changes fastest.
Arguments:
- query_rows: float32 [4096, 2240], P('tm', 'head'), may hold values from -6 to 6
- key_rows: float32 [4096, 2240], P('tm', 'head'), may hold values from -6 to 6
- value_rows: float32 [4096, 2240], P('tm', 'head'), may hold values from -6 to 6
- out_weight: float32 [2240, 2240], P(None, 'head'), may hold values from -0.125 to 0.125
- cotangent: float32 [4096, 2240], P('tm', 'head'), may hold values from -6 to 6
Outputs:
- grad_query: float32 [4096, 2240], P('tm', 'head')
- grad_key: float32 [4096, 2240], P('tm', 'head')
- grad_value: float32 [4096, 2240], P('tm', 'head')
- grad_weight: float32 [2240, 2240], P('tm', 'head')
All inputs are finite; a program needn't handle non-finite values.
Results may differ from a plain program's by a relative error of at most 0.0003.
Values sent between devices are 32-bit elements; how exact they have to be, the bound alone decides.
A program may use at most 128 MiB of HBM per device.

v0:
```python
import jax
import jax.numpy as jnp
from jax import lax
from jax.sharding import PartitionSpec as P

HEAD_DIM = 112
HIGH = lax.Precision.HIGH


def ein(spec, a, b):
    return jnp.einsum(spec, a, b, precision=HIGH, preferred_element_type=jnp.float32)


def exchange(a, axis, bit):
    return lax.ppermute(a, axis, [(i, i ^ bit) for i in range(lax.axis_size(axis))])


def scan_others(part, axis, reverse):
    count = lax.axis_size(axis)
    place = lax.axis_index(axis)
    total = part
    others = jnp.zeros_like(part)
    bit = 1
    while bit < count:
        arrived = exchange(total, axis, bit)
        below = (place & bit) != 0
        others = others + jnp.where(jnp.logical_not(below) if reverse else below, arrived, 0.0)
        total = total + arrived
        bit *= 2
    return others


def gather_xor(block, axis):
    blocks = {0: block}
    bit = lax.axis_size(axis) // 2
    while bit:
        blocks.update({k | bit: exchange(b, axis, bit) for k, b in list(blocks.items())})
        bit //= 2
    return [blocks[k] for k in range(len(blocks))]


def pieces_of(cube, order, after, held):
    place = lax.axis_index("tm")
    count = len(order)
    open_bits = list(reversed(range(count)))
    first = None
    for bit in order:
        dim = open_bits.index(bit)
        open_bits.remove(bit)
        mine = jnp.where((place & (1 << bit)) != 0, 1, 0)
        away = lax.dynamic_index_in_dim(cube, 1 - mine, dim, False)
        kept = lax.dynamic_index_in_dim(cube, mine, dim, False)
        if first is None and after is not None:
            away, _ = lax.optimization_barrier((away, after))
        if first is None and after is None:
            away, held = lax.optimization_barrier((away, held))
        arrived = exchange(away, "tm", 1 << bit)
        first = arrived if first is None else first
        cube = kept + arrived
    return cube, first, held


def shards(query_rows, key_rows, value_rows, out_weight, cotangent):
    rows = query_rows.shape[0]
    width = query_rows.shape[1]
    heads = width // HEAD_DIM
    shape_heads = (rows, heads, HEAD_DIM)
    tm = lax.axis_size("tm")
    groups = lax.axis_size("head")
    head = lax.axis_index("head")
    whole_grad = jnp.zeros((rows, groups * width), jnp.float32)
    for k, block in enumerate(gather_xor(cotangent, "head")):
        whole_grad = lax.dynamic_update_slice_in_dim(whole_grad, block, (head ^ k) * width, 1)
    grad_att = jnp.dot(whole_grad, out_weight, precision=HIGH, preferred_element_type=jnp.float32)
    query = query_rows.reshape(shape_heads).transpose(1, 0, 2)
    key = key_rows.reshape(shape_heads).transpose(1, 0, 2)
    value = value_rows.reshape(shape_heads).transpose(1, 0, 2)
    feat_q = jax.nn.relu(query)
    feat_k = jax.nn.relu(key)
    ones = jnp.ones((heads, rows, 1), jnp.float32)
    value_one = jnp.concatenate([value, ones], axis=2)
    mask = jnp.tril(jnp.ones((rows, rows), jnp.bool_))
    state = scan_others(ein("hti,htj->hij", feat_k, value_one), "tm", False)
    scores = jnp.where(mask, ein("hti,hsi->hts", feat_q, feat_k), 0.0)
    both = ein("hts,hsj->htj", scores, value_one) + ein("hti,hij->htj", feat_q, state)
    denom = 1.0 + both[:, :, HEAD_DIM:]
    attended = both[:, :, :HEAD_DIM] / denom
    flat = attended.transpose(1, 0, 2).reshape(rows, width)
    flat, grad_att = lax.optimization_barrier((flat, grad_att))
    terms = ein("tgd,tc->gdc", whole_grad.reshape(rows, tm, -1), flat)
    share = groups * width // tm
    bits = tm.bit_length() - 1
    cut = share * 2 // 40 * 8
    up = list(range(bits))
    parts = []
    arrived = None
    for low, high, order in ((0, cut, up), (cut, 2 * cut, up), (2 * cut, share, up[1:] + up[:1])):
        piece = terms[:, low:high].reshape((2,) * bits + (high - low, width))
        part, first, grad_att = pieces_of(piece, order, arrived if low == cut else None, grad_att)
        arrived = first if low == 0 else arrived
        parts.append(part)
    grad_weight = jnp.concatenate(parts, axis=0)
    grad_att = grad_att.reshape(shape_heads).transpose(1, 0, 2)
    grad_num = grad_att / denom
    grad_den = -jnp.sum(grad_att * attended, axis=2, keepdims=True) / denom
    grad_one = jnp.concatenate([grad_num, grad_den], axis=2)
    back = scan_others(ein("hti,htj->hij", feat_q, grad_one), "tm", True)
    grad_scores = jnp.where(mask, ein("htj,hsj->hts", grad_one, value_one), 0.0)
    grad_fq = ein("hts,hsi->hti", grad_scores, feat_k) + ein("htj,hij->hti", grad_one, state)
    grad_fk = ein("hts,hti->hsi", grad_scores, feat_q) + ein("hsj,hij->hsi", value_one, back)
    grad_val = ein("hts,htj->hsj", scores, grad_num) + ein(
        "hsi,hij->hsj", feat_k, back[:, :, :HEAD_DIM]
    )

    def merged(a):
        return a.transpose(1, 0, 2).reshape(rows, width)

    grad_query = merged(jnp.where(query > 0, grad_fq, 0.0))
    grad_key = merged(jnp.where(key > 0, grad_fk, 0.0))
    return (grad_query, grad_key, merged(grad_val), grad_weight)


def solution(mesh):
    return jax.shard_map(
        shards,
        mesh=mesh,
        in_specs=(
            P("tm", "head"),
            P("tm", "head"),
            P("tm", "head"),
            P(None, "head"),
            P("tm", "head"),
        ),
        out_specs=(P("tm", "head"), P("tm", "head"), P("tm", "head"), P("tm", "head")),
        check_vma=False,
    )
```

profile of v0, /device:TPU:0, one launch (start us, length us, event | category | flops | bytes accessed | tf_op | source)
XLA Modules:
  0.0 164.5 jit_solution(8386327967655833333)
XLA Ops:
  0.6 3.0 %collective-permute-start.1 = (f32[512,560]{0,1:T(8,128)}, f32[512,560]{0,1:T(8,128)}, u32[]{:S(2)}, u32[]{:S(2)}) collective-permute-start(f32[512,560]{0,1:T(8,128)} %param.9), channel_id=1, source_target_pairs={{0,2},{1,3},{2,0},{3,1},{4,6},{5,7},{6,4},{7,5},{8,10},{9,11},{10,... | collective-permute-start | bytes 3440648 | tf_op jit(solution)/shard_map/ppermute | solution.py:15
  3.7 1.4 broadcast_maximum_fusion
  5.1 0.7 fusion.25
  5.7 1.6 collective-permute-start.3
  7.3 0.1 broadcast_maximum_fusion.1
  7.4 2.3 %fusion.42 = f32[5,512,512]{2,1,0:T(8,128)S(1)} fusion(f32[5,512,112]{1,2,0:T(8,128)S(1)} %bitcast.97, f32[5,512,112]{1,2,0:T(8,128)S(1)} %bitcast.94), kind=kOutput, calls=%fused_computation.83 | convolution fusion | flops 880803840 | bytes 7536640 | tf_op jit(solution)/shard_map/hti,hsi->hts/dot_general | solution.py:11
  9.7 0.1 iota_compare_fusion
  9.8 3.9 %fusion.6 = f32[5,512,113]{1,2,0:T(8,128)} fusion(f32[5,512,512]{2,1,0:T(8,128)S(1)} %fusion.42, pred[512,512]{1,0:T(8,128)(4,1)S(1)} %iota_compare_fusion, f32[5,512,112]{1,2,0:T(8,128)S(1)} %bitcast.102), kind=kOutput, calls=%fused_computation.6 | convolution fusion | flops 889978880 | bytes 7809024 | tf_op jit(solution)/shard_map/hts,hsj->htj/dot_general | solution.py:11
  13.8 1.3 collective-permute-done.3
  15.1 1.6 collective-permute-start.4
  16.7 0.9 broadcast_compare_fusion.1
  17.6 6.1 %collective-permute-done.4 = f32[5,112,113]{2,1,0:T(8,128)S(1)} collective-permute-done((f32[5,112,113]{2,1,0:T(8,128)S(1)}, f32[5,112,113]{2,1,0:T(8,128)S(1)}, u32[]{:S(2)}, u32[]{:S(2)}) %collective-permute-start.4) | collective-permute-done | bytes 253152 | tf_op jit(solution)/shard_map/ppermute | solution.py:15
  23.7 0.8 add.131
  24.6 2.6 %collective-permute-start.5 = (f32[5,112,113]{2,1,0:T(8,128)}, f32[5,112,113]{2,1,0:T(8,128)}, u32[]{:S(2)}, u32[]{:S(2)}) collective-permute-start(f32[5,112,113]{2,1,0:T(8,128)} %add.131), channel_id=1, source_target_pairs={{0,16},{4,20},{8,24},{12,28},{16,0},{20,4},{24,8},{28,12},{1,17},{... | collective-permute-start | bytes 759368 | tf_op jit(solution)/shard_map/ppermute | solution.py:15
  27.2 0.9 broadcast_compare_fusion
  28.0 2.7 %broadcast_in_dim.32 = f32[512,2240]{0,1:T(8,128)} broadcast(f32[]{:T(128)} %constant.77.clone.1), dimensions={} | broadcast | bytes 4587524 | tf_op jit(solution)/shard_map/broadcast_in_dim | solution.py:71
  30.8 1.1 constant_dynamic-update-slice_fusion.3
  31.9 7.8 %collective-permute-done.5 = f32[5,112,113]{2,1,0:T(8,128)} collective-permute-done((f32[5,112,113]{2,1,0:T(8,128)}, f32[5,112,113]{2,1,0:T(8,128)}, u32[]{:S(2)}, u32[]{:S(2)}) %collective-permute-start.5) | collective-permute-done | bytes 253152 | tf_op jit(solution)/shard_map/ppermute | solution.py:15
  39.8 2.2 %convolution_add_fusion = f32[5,512,113]{1,2,0:T(8,128)S(1)} fusion(f32[5,512,113]{1,2,0:T(8,128)} %fusion.6, f32[5,512,112]{1,2,0:T(8,128)S(1)} %bitcast.98, f32[5,112,113]{2,1,0:T(8,128)S(1)} %select_add_fusion.1), kind=kOutput, calls=%fused_computation.16 | convolution fusion | flops 194685440 | bytes 3714240 | tf_op jit(solution)/shard_map/hti,hij->htj/dot_general | solution.py:11
  42.0 0.1 slice_divide_fusion
  42.2 2.5 %constant_dynamic-update-slice_fusion.2 = f32[512,2240]{0,1:T(8,128)} fusion(f32[512,2240]{0,1:T(8,128)} %constant_dynamic-update-slice_fusion.3, f32[512,560]{0,1:T(8,128)} %collective-permute-done, s32[]{:T(128)S(6)} %select_n.115), kind=kLoop, calls=%fused_computation.69 | loop fusion | bytes 2293764 | tf_op jit(solution)/shard_map/dynamic_update_slice | solution.py:73
  44.7 2.4 %constant_dynamic-update-slice_fusion.1 = f32[512,2240]{0,1:T(8,128)} fusion(f32[512,2240]{0,1:T(8,128)} %constant_dynamic-update-slice_fusion.2, f32[512,560]{0,1:T(8,128)} %collective-permute-done.1, s32[]{:T(128)S(6)} %select_n.116), kind=kLoop, calls=%fused_computation.68 | loop fusion | bytes 2293764 | tf_op jit(solution)/shard_map/dynamic_update_slice | solution.py:73
  47.1 1.1 constant_dynamic-update-slice_fusion
  48.2 6.8 %fusion.43 = f32[512,560]{0,1:T(8,128)S(1)} fusion(f32[512,2240]{0,1:T(8,128)} %constant_dynamic-update-slice_fusion, f32[2240,560]{0,1:T(8,128)S(1)} %bitcast.121), kind=kOutput, calls=%fused_computation.84 | convolution fusion | flops 3853516800 | bytes 10752000 | tf_op jit(solution)/shard_map/dot_general | solution.py:74
  54.9 8.4 %fusion.20 = f32[8,280,560]{2,1,0:T(8,128)S(1)} fusion(f32[512,8,280]{0,2,1:T(8,128)} %bitcast.1, f32[512,560]{0,1:T(8,128)S(1)} %bitcast.111), kind=kOutput, calls=%fused_computation.28 | convolution fusion | flops 3853516800 | bytes 10752000 | tf_op jit(solution)/shard_map/tgd,tc->gdc/dot_general | solution.py:11
  63.4 0.1 slice.26
  63.4 0.3 fusion.41
  63.8 0.1 dynamic-slice_bitcast_fusion.1
  63.9 0.3 broadcast_divide_fusion
  64.2 1.3 slice-done
  65.5 0.3 slice-done.1
  65.8 0.1 copy-done.3
  66.0 2.1 %fusion.4 = f32[5,512,112]{1,2,0:T(8,128)S(1)} fusion(f32[5,512,112]{1,2,0:T(8,128)S(1)} %get-tuple-element.20, f32[5,512,512]{2,1,0:T(8,128)S(1)} %bitcast.92, pred[512,512]{1,0:T(8,128)(4,1)S(1)} %copy-done.3), kind=kOutput, calls=%fused_computation.4 | convolution fusion | flops 882114560 | bytes 7798784 | tf_op jit(solution)/shard_map/hts,htj->hsj/dot_general | solution.py:11
  68.1 0.8 fusion.28
  68.9 2.4 %fusion.23 = f32[5,512,512]{2,1,0:T(8,128)S(1)} fusion(f32[5,512,112]{1,2,0:T(8,128)S(1)} %bitcast.103, f32[5,512,1]{1,2,0:T(1,128)S(1)} %reshape_divide_fusion, f32[5,512,112]{1,2,0:T(8,128)S(1)} %get-tuple-element.20), kind=kOutput, calls=%fused_computation.34 | convolution fusion | flops 888957440 | bytes 7546880 | tf_op jit(solution)/shard_map/htj,hsj->hts/dot_general | solution.py:11
  71.2 2.7 %collective-permute-start.6 = (f32[5,112,113]{2,1,0:T(8,128)S(1)}, f32[5,112,113]{2,1,0:T(8,128)S(1)}, u32[]{:S(2)}, u32[]{:S(2)}) collective-permute-start(f32[5,112,113]{2,1,0:T(8,128)S(1)} %fusion.28), channel_id=1, source_target_pairs={{0,4},{4,0},{8,12},{12,8},{16,20},{20,16},{24,28},{28,24},{1,5},{5... | collective-permute-start | bytes 759368 | tf_op jit(solution)/shard_map/ppermute | solution.py:15
  73.9 0.8 collective-permute-start.15
  74.7 2.0 %fusion = f32[5,512,112]{1,2,0:T(8,128)S(1)} fusion(f32[5,512,112]{1,2,0:T(8,128)S(1)} %bitcast.100, f32[5,512,512]{2,1,0:T(8,128)S(1)} %fusion.23, pred[512,512]{1,0:T(8,128)(4,1)S(1)} %copy-done.3), kind=kOutput, calls=%fused_computation | convolution fusion | flops 882114560 | bytes 7798784 | tf_op jit(solution)/shard_map/hts,hti->hsi/dot_general | solution.py:11
  76.7 2.9 %fusion.2 = f32[5,512,112]{1,2,0:T(8,128)S(1)} fusion(f32[5,512,112]{1,2,0:T(8,128)S(1)} %bitcast.95, f32[5,512,512]{2,1,0:T(8,128)S(1)} %fusion.23, pred[512,512]{1,0:T(8,128)(4,1)S(1)} %copy-done.3), kind=kOutput, calls=%fused_computation.2 | convolution fusion | flops 882114560 | bytes 7798784 | tf_op jit(solution)/shard_map/hts,hsi->hti/dot_general | solution.py:11
  79.6 0.5 collective-permute-start.9
  80.3 1.8 %collective-permute-start.7 = (f32[5,112,113]{2,1,0:T(8,128)S(1)}, f32[5,112,113]{2,1,0:T(8,128)S(1)}, u32[]{:S(2)}, u32[]{:S(2)}) collective-permute-start(f32[5,112,113]{2,1,0:T(8,128)S(1)} %add.139), channel_id=1, source_target_pairs={{0,8},{4,12},{8,0},{12,4},{16,24},{20,28},{24,16},{28,20},{1,9},{5... | collective-permute-start | bytes 759368 | tf_op jit(solution)/shard_map/ppermute | solution.py:15
  82.0 7.8 %collective-permute-done.15 = f32[2,2,56,560]{3,2,1,0:T(8,128)S(1)} collective-permute-done((f32[2,2,56,560]{3,2,1,0:T(8,128)S(1)}, f32[2,2,56,560]{3,2,1,0:T(8,128)S(1)}, u32[]{:S(2)}, u32[]{:S(2)}) %collective-permute-start.15) | collective-permute-done | bytes 501792 | tf_op jit(solution)/shard_map/ppermute | solution.py:15
  89.9 2.2 %collective-permute-start.16 = (f32[2,56,560]{2,1,0:T(8,128)S(1)}, f32[2,56,560]{2,1,0:T(8,128)S(1)}, u32[]{:S(2)}, u32[]{:S(2)}) collective-permute-start(f32[2,56,560]{2,1,0:T(8,128)S(1)} %dynamic-slice_bitcast_fusion.5), channel_id=1, source_target_pairs={{0,16},{4,20},{8,24},{12,28},{16,0},{20,4},{24,8},{28,12},{1,17},{... | collective-permute-start | bytes 752648 | tf_op jit(solution)/shard_map/ppermute | solution.py:15
  92.1 1.8 %fusion.18 = f32[512,5,112]{0,2,1:T(8,128)} fusion(pred[512,5,112]{0,2,1:T(8,128)(4,1)S(1)} %bitcast.114, f32[5,512,112]{1,2,0:T(8,128)S(1)} %fusion.2, f32[5,112,113]{2,1,0:T(8,128)S(1)} %select_add_fusion.1, f32[5,512,1]{1,2,0:T(1,128)S(1)} %reshape_divide_fusion, f32[5,512,112]{1,2,0:T(8,128)S(1)} %get-tuple-element.20), kind=kOutput, calls=%fused_computation.22 | convolution fusion | flops 195258880 | bytes 3990720 | tf_op jit(solution)/shard_map/htj,hij->hti/dot_general | solution.py:11
  93.9 5.1 %collective-permute-done.7 = f32[5,112,113]{2,1,0:T(8,128)S(1)} collective-permute-done((f32[5,112,113]{2,1,0:T(8,128)S(1)}, f32[5,112,113]{2,1,0:T(8,128)S(1)}, u32[]{:S(2)}, u32[]{:S(2)}) %collective-permute-start.7) | collective-permute-done | bytes 253152 | tf_op jit(solution)/shard_map/ppermute | solution.py:15
  99.0 0.1 collective-permute-start.8
  99.1 11.5 %collective-permute-done.16 = f32[2,56,560]{2,1,0:T(8,128)S(1)} collective-permute-done((f32[2,56,560]{2,1,0:T(8,128)S(1)}, f32[2,56,560]{2,1,0:T(8,128)S(1)}, u32[]{:S(2)}, u32[]{:S(2)}) %collective-permute-start.16) | collective-permute-done | bytes 250912 | tf_op jit(solution)/shard_map/ppermute | solution.py:15
  110.7 0.1 collective-permute-start.12
  110.8 2.0 %collective-permute-start.17 = (f32[56,560]{1,0:T(8,128)S(1)}, f32[56,560]{1,0:T(8,128)S(1)}, u32[]{:S(2)}, u32[]{:S(2)}) collective-permute-start(f32[56,560]{1,0:T(8,128)S(1)} %dynamic-slice_bitcast_fusion.8), channel_id=1, source_target_pairs={{0,4},{4,0},{8,12},{12,8},{16,20},{20,16},{24,28},{28,24},{1,5},{5... | collective-permute-start | bytes 376328 | tf_op jit(solution)/shard_map/ppermute | solution.py:15
  112.9 3.1 %collective-permute-done.8 = f32[5,112,113]{2,1,0:T(8,128)S(1)} collective-permute-done((f32[5,112,113]{2,1,0:T(8,128)S(1)}, f32[5,112,113]{2,1,0:T(8,128)S(1)}, u32[]{:S(2)}, u32[]{:S(2)}) %collective-permute-start.8) | collective-permute-done | bytes 253152 | tf_op jit(solution)/shard_map/ppermute | solution.py:15
  116.1 1.7 %convolution_add_fusion.1 = f32[5,512,112]{1,2,0:T(8,128)} fusion(f32[5,512,112]{1,2,0:T(8,128)S(1)} %fusion.4, f32[5,512,112]{1,2,0:T(8,128)S(1)} %bitcast.96, f32[5,112,113]{2,1,0:T(8,128)S(1)} %select_add_fusion), kind=kOutput, calls=%fused_computation.17 | convolution fusion | flops 192962560 | bytes 3693760 | tf_op jit(solution)/shard_map/hsi,hij->hsj/dot_general | solution.py:11
  117.8 0.2 bitcast_add_fusion.1
  118.0 0.6 collective-permute-start.10
  118.5 14.9 %collective-permute-done.12 = f32[2,2,112,560]{3,2,1,0:T(8,128)S(1)} collective-permute-done((f32[2,2,112,560]{3,2,1,0:T(8,128)S(1)}, f32[2,2,112,560]{3,2,1,0:T(8,128)S(1)}, u32[]{:S(2)}, u32[]{:S(2)}) %collective-permute-start.12) | collective-permute-done | bytes 1003552 | tf_op jit(solution)/shard_map/ppermute | solution.py:15
  133.5 0.1 bitcast_add_fusion
  133.7 3.5 %collective-permute-start.13 = (f32[2,112,560]{2,1,0:T(8,128)S(1)}, f32[2,112,560]{2,1,0:T(8,128)S(1)}, u32[]{:S(2)}, u32[]{:S(2)}) collective-permute-start(f32[2,112,560]{2,1,0:T(8,128)S(1)} %dynamic-slice_bitcast_fusion.2), channel_id=1, source_target_pairs={{0,8},{4,12},{8,0},{12,4},{16,24},{20,28},{24,16},{28,20},{1,9},{5... | collective-permute-start | bytes 1505288 | tf_op jit(solution)/shard_map/ppermute | solution.py:15
  137.2 1.7 %fusion.19 = f32[512,5,112]{0,2,1:T(8,128)} fusion(pred[512,5,112]{0,2,1:T(8,128)(4,1)S(1)} %bitcast.117, f32[5,512,112]{1,2,0:T(8,128)S(1)} %fusion, f32[5,112,113]{2,1,0:T(8,128)S(1)} %select_add_fusion, f32[5,512,112]{1,2,0:T(8,128)S(1)} %bitcast.104), kind=kOutput, calls=%fused_computation.23 | convolution fusion | flops 194969600 | bytes 3980480 | tf_op jit(solution)/shard_map/hsj,hij->hsi/dot_general | solution.py:11
  138.9 0.1 bitcast_add_fusion.4
  139.0 3.4 %collective-permute-start.11 = (f32[112,560]{1,0:T(8,128)S(1)}, f32[112,560]{1,0:T(8,128)S(1)}, u32[]{:S(2)}, u32[]{:S(2)}) collective-permute-start(f32[112,560]{1,0:T(8,128)S(1)} %dynamic-slice_bitcast_fusion.7), channel_id=1, source_target_pairs={{0,16},{4,20},{8,24},{12,28},{16,0},{20,4},{24,8},{28,12},{1,17},{... | collective-permute-start | bytes 752648 | tf_op jit(solution)/shard_map/ppermute | solution.py:15
  142.5 8.7 %collective-permute-done.13 = f32[2,112,560]{2,1,0:T(8,128)S(1)} collective-permute-done((f32[2,112,560]{2,1,0:T(8,128)S(1)}, f32[2,112,560]{2,1,0:T(8,128)S(1)}, u32[]{:S(2)}, u32[]{:S(2)}) %collective-permute-start.13) | collective-permute-done | bytes 501792 | tf_op jit(solution)/shard_map/ppermute | solution.py:15
  151.2 0.1 bitcast_add_fusion.3
  151.3 2.6 %collective-permute-start.14 = (f32[112,560]{1,0:T(8,128)S(1)}, f32[112,560]{1,0:T(8,128)S(1)}, u32[]{:S(2)}, u32[]{:S(2)}) collective-permute-start(f32[112,560]{1,0:T(8,128)S(1)} %dynamic-slice_bitcast_fusion.6), channel_id=1, source_target_pairs={{0,16},{4,20},{8,24},{12,28},{16,0},{20,4},{24,8},{28,12},{1,17},{... | collective-permute-start | bytes 752648 | tf_op jit(solution)/shard_map/ppermute | solution.py:15
  154.0 9.6 %collective-permute-done.14 = f32[112,560]{1,0:T(8,128)S(1)} collective-permute-done((f32[112,560]{1,0:T(8,128)S(1)}, f32[112,560]{1,0:T(8,128)S(1)}, u32[]{:S(2)}, u32[]{:S(2)}) %collective-permute-start.14) | collective-permute-done | bytes 250912 | tf_op jit(solution)/shard_map/ppermute | solution.py:15
  163.6 0.9 pad_maximum_fusion.4
  (61 shorter events, 0.9 us)
Async XLA Ops:
  0.6 4.4 %copy-start.1 = (f32[512,560]{0,1:T(8,128)S(1)}, f32[512,560]{0,1:T(8,128)}, u32[]{:S(2)}) copy-start(f32[512,560]{0,1:T(8,128)} %param.7) | copy-start | bytes 3440644
  0.6 31.3 %collective-permute-start.1 = (f32[512,560]{0,1:T(8,128)}, f32[512,560]{0,1:T(8,128)}, u32[]{:S(2)}, u32[]{:S(2)}) collective-permute-start(f32[512,560]{0,1:T(8,128)} %param.9), channel_id=1, source_target_pairs={{0,2},{1,3},{2,0},{3,1},{4,6},{5,7},{6,4},{7,5},{8,10},{9,11},{10,... | collective-permute-start | bytes 3440648 | tf_op jit(solution)/shard_map/ppermute | solution.py:15
  3.7 38.5 %collective-permute-start = (f32[512,560]{0,1:T(8,128)}, f32[512,560]{0,1:T(8,128)}, u32[]{:S(2)}, u32[]{:S(2)}) collective-permute-start(f32[512,560]{0,1:T(8,128)} %param.9), channel_id=1, source_target_pairs={{0,1},{1,0},{2,3},{3,2},{4,5},{5,4},{6,7},{7,6},{8,9},{9,8},{10,11... | collective-permute-start | bytes 3440648 | tf_op jit(solution)/shard_map/ppermute | solution.py:15
  5.1 2.2 %copy-start.4 = (f32[512,560]{0,1:T(8,128)S(1)}, f32[512,560]{0,1:T(8,128)}, u32[]{:S(2)}) copy-start(f32[512,560]{0,1:T(8,128)} %param.5) | copy-start | bytes 3440644
  5.7 9.3 %collective-permute-start.3 = (f32[5,112,113]{2,1,0:T(8,128)S(1)}, f32[5,112,113]{2,1,0:T(8,128)S(1)}, u32[]{:S(2)}, u32[]{:S(2)}) collective-permute-start(f32[5,112,113]{2,1,0:T(8,128)S(1)} %fusion.25), channel_id=1, source_target_pairs={{0,4},{4,0},{8,12},{12,8},{16,20},{20,16},{24,28},{28,24},{1,5},{5... | collective-permute-start | bytes 759368 | tf_op jit(solution)/shard_map/ppermute | solution.py:15
  9.7 4.0 %copy-start = (f32[5,512,512]{2,1,0:T(8,128)}, f32[5,512,512]{2,1,0:T(8,128)S(1)}, u32[]{:S(2)}) copy-start(f32[5,512,512]{2,1,0:T(8,128)S(1)} %fusion.42) | copy-start | bytes 15728644
  9.8 3.9 %copy-start.2 = (pred[512,512]{1,0:T(8,128)(4,1)}, pred[512,512]{1,0:T(8,128)(4,1)S(1)}, u32[]{:S(2)}) copy-start(pred[512,512]{1,0:T(8,128)(4,1)S(1)} %iota_compare_fusion) | copy-start | bytes 786436
  15.0 2.6 %copy-start.8 = (f32[5,112,113]{2,1,0:T(8,128)}, f32[5,112,113]{2,1,0:T(8,128)S(1)}, u32[]{:S(2)}) copy-start(f32[5,112,113]{2,1,0:T(8,128)S(1)} %collective-permute-done.3) | copy-start | bytes 759364
  15.1 12.1 %copy-start.5 = (f32[512,560]{0,1:T(8,128)S(1)}, f32[512,560]{0,1:T(8,128)}, u32[]{:S(2)}) copy-start(f32[512,560]{0,1:T(8,128)} %param.6) | copy-start | bytes 3440644
  15.1 8.6 %collective-permute-start.4 = (f32[5,112,113]{2,1,0:T(8,128)S(1)}, f32[5,112,113]{2,1,0:T(8,128)S(1)}, u32[]{:S(2)}, u32[]{:S(2)}) collective-permute-start(f32[5,112,113]{2,1,0:T(8,128)S(1)} %add.129), channel_id=1, source_target_pairs={{0,8},{4,12},{8,0},{12,4},{16,24},{20,28},{24,16},{28,20},{1,9},{5... | collective-permute-start | bytes 759368 | tf_op jit(solution)/shard_map/ppermute | solution.py:15
  23.7 4.3 %copy-start.9 = (f32[5,112,113]{2,1,0:T(8,128)}, f32[5,112,113]{2,1,0:T(8,128)S(1)}, u32[]{:S(2)}) copy-start(f32[5,112,113]{2,1,0:T(8,128)S(1)} %collective-permute-done.4) | copy-start | bytes 759364
  24.6 15.2 %collective-permute-start.5 = (f32[5,112,113]{2,1,0:T(8,128)}, f32[5,112,113]{2,1,0:T(8,128)}, u32[]{:S(2)}, u32[]{:S(2)}) collective-permute-start(f32[5,112,113]{2,1,0:T(8,128)} %add.131), channel_id=1, source_target_pairs={{0,16},{4,20},{8,24},{12,28},{16,0},{20,4},{24,8},{28,12},{1,17},{... | collective-permute-start | bytes 759368 | tf_op jit(solution)/shard_map/ppermute | solution.py:15
  28.0 2.7 %copy-start.6 = (f32[512,560]{0,1:T(8,128)S(1)}, f32[512,560]{0,1:T(8,128)}, u32[]{:S(2)}) copy-start(f32[512,560]{0,1:T(8,128)} %param.9) | copy-start | bytes 3440644
  31.9 15.2 %collective-permute-start.2 = (f32[512,560]{0,1:T(8,128)}, f32[512,560]{0,1:T(8,128)S(1)}, u32[]{:S(2)}, u32[]{:S(2)}) collective-permute-start(f32[512,560]{0,1:T(8,128)} %collective-permute-done.1), channel_id=1, source_target_pairs={{0,1},{1,0},{2,3},{3,2},{4,5},{5,4},{6,7},{7,6},{8,9},{9,8},{10,11... | collective-permute-start | bytes 3440648 | tf_op jit(solution)/shard_map/ppermute | solution.py:15
  39.7 8.4 %slice-start.2 = ((s8[5160960]{0:T(1024)(128)(4,1)}), s8[4194304]{0:T(1024)(128)(4,1)S(1)}, s32[]{:S(2)}) async-start(s8[5160960]{0:T(1024)(128)(4,1)} %bitcast.120), calls=%async_computation.2 | async-start | bytes 8388608
  42.0 6.1 %slice-start.3 = ((s8[5160960]{0:T(1024)(128)(4,1)}), s8[966656]{0:T(1024)(128)(4,1)S(1)}, s32[]{:S(2)}) async-start(s8[5160960]{0:T(1024)(128)(4,1)} %bitcast.120), calls=%async_computation.3 | async-start | bytes 1933312
  63.3 2.2 %slice-start = ((s8[5242880]{0:T(1024)(128)(4,1)}), s8[4194304]{0:T(1024)(128)(4,1)S(1)}, s32[]{:S(2)}) async-start(s8[5242880]{0:T(1024)(128)(4,1)} %bitcast.91), calls=%async_computation | async-start | bytes 8388608
  63.4 2.4 %slice-start.1 = ((s8[5242880]{0:T(1024)(128)(4,1)}), s8[1048576]{0:T(1024)(128)(4,1)S(1)}, s32[]{:S(2)}) async-start(s8[5242880]{0:T(1024)(128)(4,1)} %bitcast.91), calls=%async_computation.1 | async-start | bytes 2097152
  63.9 2.1 %copy-start.3 = (pred[512,512]{1,0:T(8,128)(4,1)S(1)}, pred[512,512]{1,0:T(8,128)(4,1)}, u32[]{:S(2)}) copy-start(pred[512,512]{1,0:T(8,128)(4,1)} %copy-done.2) | copy-start | bytes 786436
  71.2 8.9 %collective-permute-start.6 = (f32[5,112,113]{2,1,0:T(8,128)S(1)}, f32[5,112,113]{2,1,0:T(8,128)S(1)}, u32[]{:S(2)}, u32[]{:S(2)}) collective-permute-start(f32[5,112,113]{2,1,0:T(8,128)S(1)} %fusion.28), channel_id=1, source_target_pairs={{0,4},{4,0},{8,12},{12,8},{16,20},{20,16},{24,28},{28,24},{1,5},{5... | collective-permute-start | bytes 759368 | tf_op jit(solution)/shard_map/ppermute | solution.py:15
  73.9 15.9 %collective-permute-start.15 = (f32[2,2,56,560]{3,2,1,0:T(8,128)S(1)}, f32[2,2,56,560]{3,2,1,0:T(8,128)S(1)}, u32[]{:S(2)}, u32[]{:S(2)}) collective-permute-start(f32[2,2,56,560]{3,2,1,0:T(8,128)S(1)} %dynamic-slice_bitcast_fusion.4), channel_id=1, source_target_pairs={{0,8},{4,12},{8,0},{12,4},{16,24},{20,28},{24,16},{28,20},{1,9},{5... | collective-permute-start | bytes 1505288 | tf_op jit(solution)/shard_map/ppermute | solution.py:15
  79.6 31.1 %collective-permute-start.9 = (f32[2,2,112,560]{3,2,1,0:T(8,128)S(1)}, f32[2,2,112,560]{3,2,1,0:T(8,128)S(1)}, u32[]{:S(2)}, u32[]{:S(2)}) collective-permute-start(f32[2,2,112,560]{3,2,1,0:T(8,128)S(1)} %dynamic-slice_bitcast_fusion.1), channel_id=1, source_target_pairs={{0,4},{4,0},{8,12},{12,8},{16,20},{20,16},{24,28},{28,24},{1,5},{5... | collective-permute-start | bytes 3010568 | tf_op jit(solution)/shard_map/ppermute | solution.py:15
  80.2 11.9 %copy-start.7 = (pred[512,560]{0,1:T(8,128)(4,1)S(1)}, pred[512,560]{0,1:T(8,128)(4,1)}, u32[]{:S(2)}) copy-start(pred[512,560]{0,1:T(8,128)(4,1)} %broadcast_compare_fusion.1) | copy-start | bytes 860164
  80.3 18.7 %collective-permute-start.7 = (f32[5,112,113]{2,1,0:T(8,128)S(1)}, f32[5,112,113]{2,1,0:T(8,128)S(1)}, u32[]{:S(2)}, u32[]{:S(2)}) collective-permute-start(f32[5,112,113]{2,1,0:T(8,128)S(1)} %add.139), channel_id=1, source_target_pairs={{0,8},{4,12},{8,0},{12,4},{16,24},{20,28},{24,16},{28,20},{1,9},{5... | collective-permute-start | bytes 759368 | tf_op jit(solution)/shard_map/ppermute | solution.py:15
  89.9 20.7 %collective-permute-start.16 = (f32[2,56,560]{2,1,0:T(8,128)S(1)}, f32[2,56,560]{2,1,0:T(8,128)S(1)}, u32[]{:S(2)}, u32[]{:S(2)}) collective-permute-start(f32[2,56,560]{2,1,0:T(8,128)S(1)} %dynamic-slice_bitcast_fusion.5), channel_id=1, source_target_pairs={{0,16},{4,20},{8,24},{12,28},{16,0},{20,4},{24,8},{28,12},{1,17},{... | collective-permute-start | bytes 752648 | tf_op jit(solution)/shard_map/ppermute | solution.py:15
  99.0 17.0 %collective-permute-start.8 = (f32[5,112,113]{2,1,0:T(8,128)S(1)}, f32[5,112,113]{2,1,0:T(8,128)S(1)}, u32[]{:S(2)}, u32[]{:S(2)}) collective-permute-start(f32[5,112,113]{2,1,0:T(8,128)S(1)} %add.141), channel_id=1, source_target_pairs={{0,16},{4,20},{8,24},{12,28},{16,0},{20,4},{24,8},{28,12},{1,17},{... | collective-permute-start | bytes 759368 | tf_op jit(solution)/shard_map/ppermute | solution.py:15
  110.7 22.8 %collective-permute-start.12 = (f32[2,2,112,560]{3,2,1,0:T(8,128)S(1)}, f32[2,2,112,560]{3,2,1,0:T(8,128)S(1)}, u32[]{:S(2)}, u32[]{:S(2)}) collective-permute-start(f32[2,2,112,560]{3,2,1,0:T(8,128)S(1)} %dynamic-slice_bitcast_fusion), channel_id=1, source_target_pairs={{0,4},{4,0},{8,12},{12,8},{16,20},{20,16},{24,28},{28,24},{1,5},{5... | collective-permute-start | bytes 3010568 | tf_op jit(solution)/shard_map/ppermute | solution.py:15
  110.8 43.1 %collective-permute-start.17 = (f32[56,560]{1,0:T(8,128)S(1)}, f32[56,560]{1,0:T(8,128)S(1)}, u32[]{:S(2)}, u32[]{:S(2)}) collective-permute-start(f32[56,560]{1,0:T(8,128)S(1)} %dynamic-slice_bitcast_fusion.8), channel_id=1, source_target_pairs={{0,4},{4,0},{8,12},{12,8},{16,20},{20,16},{24,28},{28,24},{1,5},{5... | collective-permute-start | bytes 376328 | tf_op jit(solution)/shard_map/ppermute | solution.py:15
  118.0 20.9 %collective-permute-start.10 = (f32[2,112,560]{2,1,0:T(8,128)S(1)}, f32[2,112,560]{2,1,0:T(8,128)S(1)}, u32[]{:S(2)}, u32[]{:S(2)}) collective-permute-start(f32[2,112,560]{2,1,0:T(8,128)S(1)} %dynamic-slice_bitcast_fusion.3), channel_id=1, source_target_pairs={{0,8},{4,12},{8,0},{12,4},{16,24},{20,28},{24,16},{28,20},{1,9},{5... | collective-permute-start | bytes 1505288 | tf_op jit(solution)/shard_map/ppermute | solution.py:15
  133.6 3.6 %copy-start.10 = (pred[512,560]{0,1:T(8,128)(4,1)S(1)}, pred[512,560]{0,1:T(8,128)(4,1)}, u32[]{:S(2)}) copy-start(pred[512,560]{0,1:T(8,128)(4,1)} %broadcast_compare_fusion) | copy-start | bytes 860164
  133.7 17.5 %collective-permute-start.13 = (f32[2,112,560]{2,1,0:T(8,128)S(1)}, f32[2,112,560]{2,1,0:T(8,128)S(1)}, u32[]{:S(2)}, u32[]{:S(2)}) collective-permute-start(f32[2,112,560]{2,1,0:T(8,128)S(1)} %dynamic-slice_bitcast_fusion.2), channel_id=1, source_target_pairs={{0,8},{4,12},{8,0},{12,4},{16,24},{20,28},{24,16},{28,20},{1,9},{5... | collective-permute-start | bytes 1505288 | tf_op jit(solution)/shard_map/ppermute | solution.py:15
  139.0 14.9 %collective-permute-start.11 = (f32[112,560]{1,0:T(8,128)S(1)}, f32[112,560]{1,0:T(8,128)S(1)}, u32[]{:S(2)}, u32[]{:S(2)}) collective-permute-start(f32[112,560]{1,0:T(8,128)S(1)} %dynamic-slice_bitcast_fusion.7), channel_id=1, source_target_pairs={{0,16},{4,20},{8,24},{12,28},{16,0},{20,4},{24,8},{28,12},{1,17},{... | collective-permute-start | bytes 752648 | tf_op jit(solution)/shard_map/ppermute | solution.py:15
  151.3 12.3 %collective-permute-start.14 = (f32[112,560]{1,0:T(8,128)S(1)}, f32[112,560]{1,0:T(8,128)S(1)}, u32[]{:S(2)}, u32[]{:S(2)}) collective-permute-start(f32[112,560]{1,0:T(8,128)S(1)} %dynamic-slice_bitcast_fusion.6), channel_id=1, source_target_pairs={{0,16},{4,20},{8,24},{12,28},{16,0},{20,4},{24,8},{28,12},{1,17},{... | collective-permute-start | bytes 752648 | tf_op jit(solution)/shard_map/ppermute | solution.py:15
where the time goes:
time: 165 us
  waiting for transfers between devices  76.1 us (46%)
  matrix products  39.5 us (24%)
  starting transfers between devices  29.1 us (18%)
  local copies, waits for them, and re-layouts  12.4 us (8%)
  other arithmetic  6.35 us (4%)
    ppermute x18, waiting for transfers between devices, exchange(): lax.ppermute(a, axis, [(i, i ^ bit) for i in range(lax.axis_size(axis))])  76.1 us
    dot_general x13, matrix products, ein(): jnp.einsum(spec, a, b, precision=HIGH, preferred_element_type=jnp.float32)  32.8 us
    ppermute x18, starting transfers between devices, exchange(): lax.ppermute(a, axis, [(i, i ^ bit) for i in range(lax.axis_size(axis))])  29.1 us
    dynamic_update_slice x4, local copies, waits for them, and re-layouts, shards(): lax.dynamic_update_slice_in_dim(whole_grad, block, (head ^ k) * width, 1)  7.11 us
    dot_general x1, matrix products, shards(): jnp.dot(whole_grad, out_weight, precision=HIGH, preferred_element_type=jn...  6.77 us
  transfers between devices with their start and end apart: 18, of which 10 were waited for; matrix products, arithmetic and copies ran while one was open for 20% of the time, Pallas kernels for 0%

commit v1 on v0

--- a/solution.py
+++ b/solution.py
@@ -39,25 +39,22 @@
     return [blocks[k] for k in range(len(blocks))]
 
 
-def pieces_of(cube, order, after, held):
-    place = lax.axis_index("tm")
-    count = len(order)
-    open_bits = list(reversed(range(count)))
-    first = None
+def split(cube, left, bit):
+    dim = left.index(bit)
+    mine = jnp.where((lax.axis_index("tm") & (1 << bit)) != 0, 1, 0)
+    away = lax.dynamic_index_in_dim(cube, 1 - mine, dim, False)
+    kept = lax.dynamic_index_in_dim(cube, mine, dim, False)
+    return away, kept, [x for x in left if x != bit]
+
+
+def finish(cube, left, order, gate):
     for bit in order:
-        dim = open_bits.index(bit)
-        open_bits.remove(bit)
-        mine = jnp.where((place & (1 << bit)) != 0, 1, 0)
-        away = lax.dynamic_index_in_dim(cube, 1 - mine, dim, False)
-        kept = lax.dynamic_index_in_dim(cube, mine, dim, False)
-        if first is None and after is not None:
-            away, _ = lax.optimization_barrier((away, after))
-        if first is None and after is None:
-            away, held = lax.optimization_barrier((away, held))
-        arrived = exchange(away, "tm", 1 << bit)
-        first = arrived if first is None else first
-        cube = kept + arrived
-    return cube, first, held
+        away, kept, left = split(cube, left, bit)
+        if gate is not None:
+            away, _ = lax.optimization_barrier((away, gate))
+            gate = None
+        cube = kept + exchange(away, "tm", 1 << bit)
+    return cube
 
 
 def shards(query_rows, key_rows, value_rows, out_weight, cotangent):
@@ -71,7 +68,6 @@
     whole_grad = jnp.zeros((rows, groups * width), jnp.float32)
     for k, block in enumerate(gather_xor(cotangent, "head")):
         whole_grad = lax.dynamic_update_slice_in_dim(whole_grad, block, (head ^ k) * width, 1)
-    grad_att = jnp.dot(whole_grad, out_weight, precision=HIGH, preferred_element_type=jnp.float32)
     query = query_rows.reshape(shape_heads).transpose(1, 0, 2)
     key = key_rows.reshape(shape_heads).transpose(1, 0, 2)
     value = value_rows.reshape(shape_heads).transpose(1, 0, 2)
@@ -86,26 +82,35 @@
     denom = 1.0 + both[:, :, HEAD_DIM:]
     attended = both[:, :, :HEAD_DIM] / denom
     flat = attended.transpose(1, 0, 2).reshape(rows, width)
-    flat, grad_att = lax.optimization_barrier((flat, grad_att))
     terms = ein("tgd,tc->gdc", whole_grad.reshape(rows, tm, -1), flat)
     share = groups * width // tm
     bits = tm.bit_length() - 1
     cut = share * 2 // 40 * 8
     up = list(range(bits))
-    parts = []
-    arrived = None
-    for low, high, order in ((0, cut, up), (cut, 2 * cut, up), (2 * cut, share, up[1:] + up[:1])):
-        piece = terms[:, low:high].reshape((2,) * bits + (high - low, width))
-        part, first, grad_att = pieces_of(piece, order, arrived if low == cut else None, grad_att)
-        arrived = first if low == 0 else arrived
-        parts.append(part)
-    grad_weight = jnp.concatenate(parts, axis=0)
+    around = up[1:] + up[:1]
+    left = up[::-1]
+
+    def cube_of(low, high):
+        return terms[:, low:high].reshape((2,) * bits + (high - low, width))
+
+    away_a, kept_a, left_a = split(cube_of(0, cut), left, up[0])
+    away_c, kept_c, left_c = split(cube_of(2 * cut, share), left, around[0])
+    away_a, away_c, whole_late = lax.optimization_barrier((away_a, away_c, whole_grad))
+    arrived_a = exchange(away_a, "tm", 1 << up[0])
+    arrived_c = exchange(away_c, "tm", 1 << around[0])
+    grad_att = jnp.dot(whole_late, out_weight, precision=HIGH, preferred_element_type=jnp.float32)
+    grad_att, arrived_c = lax.optimization_barrier((grad_att, arrived_c))
+    part_b = finish(cube_of(cut, 2 * cut), left, up, arrived_a)
+    part_a = finish(kept_a + arrived_a, left_a, up[1:], None)
+    part_c = finish(kept_c + arrived_c, left_c, around[1:], arrived_a)
+    grad_weight = jnp.concatenate([part_a, part_b, part_c], axis=0)
     grad_att = grad_att.reshape(shape_heads).transpose(1, 0, 2)
     grad_num = grad_att / denom
     grad_den = -jnp.sum(grad_att * attended, axis=2, keepdims=True) / denom
     grad_one = jnp.concatenate([grad_num, grad_den], axis=2)
     back = scan_others(ein("hti,htj->hij", feat_q, grad_one), "tm", True)
     grad_scores = jnp.where(mask, ein("htj,hsj->hts", grad_one, value_one), 0.0)
+    grad_scores, scores, _ = lax.optimization_barrier((grad_scores, scores, arrived_a))
     grad_fq = ein("hts,hsi->hti", grad_scores, feat_k) + ein("htj,hij->hti", grad_one, state)
     grad_fk = ein("hts,hti->hsi", grad_scores, feat_q) + ein("hsj,hij->hsi", value_one, back)
     grad_val = ein("hts,htj->hsj", scores, grad_num) + ein(

time: 165 us -> 162 us (0.982)
  transfers between devices with their start and end apart: 18 -> 18, of which waited for: 10 -> 10; matrix products, arithmetic and copies ran while one was open for 20% -> 28% of each run, Pallas kernels for 0% -> 0%
where the time goes in v1:
time: 162 us
  waiting for transfers between devices  76.4 us (47%)
  matrix products  38.2 us (24%)
  starting transfers between devices  28.5 us (18%)
  local copies, waits for them, and re-layouts  11.2 us (7%)
  other arithmetic  6.38 us (4%)
    ppermute x18, waiting for transfers between devices, exchange(): lax.ppermute(a, axis, [(i, i ^ bit) for i in range(lax.axis_size(axis))])  76.4 us
    dot_general x13, matrix products, ein(): jnp.einsum(spec, a, b, precision=HIGH, preferred_element_type=jnp.float32)  31.2 us
    ppermute x18, starting transfers between devices, exchange(): lax.ppermute(a, axis, [(i, i ^ bit) for i in range(lax.axis_size(axis))])  28.5 us
    dynamic_update_slice x4, local copies, waits for them, and re-layouts, shards(): lax.dynamic_update_slice_in_dim(whole_grad, block, (head ^ k) * width, 1)  7.03 us
    dot_general x1, matrix products, shards(): jnp.dot(whole_late, out_weight, precision=HIGH, preferred_element_type=jn...  6.96 us
  transfers between devices with their start and end apart: 18, of which 10 were waited for; matrix products, arithmetic and copies ran while one was open for 28% of the time, Pallas kernels for 0%

profile of v1, /device:TPU:0, one launch (start us, length us, event | category | flops | bytes accessed | tf_op | source)
XLA Modules:
  0.0 161.8 jit_solution(7543476756041876228)
XLA Ops:
  0.6 3.0 %collective-permute-start.1 = (f32[512,560]{0,1:T(8,128)}, f32[512,560]{0,1:T(8,128)}, u32[]{:S(2)}, u32[]{:S(2)}) collective-permute-start(f32[512,560]{0,1:T(8,128)} %param.9), channel_id=1, source_target_pairs={{0,2},{1,3},{2,0},{3,1},{4,6},{5,7},{6,4},{7,5},{8,10},{9,11},{10,... | collective-permute-start | bytes 3440648 | tf_op jit(solution)/shard_map/ppermute | solution.py:15
  3.7 1.4 broadcast_maximum_fusion
  5.1 0.7 fusion.7
  5.7 1.6 collective-permute-start.3
  7.3 0.1 iota_compare_fusion
  7.4 0.1 broadcast_maximum_fusion.1
  7.5 0.6 copy-done.4
  8.1 2.7 %broadcast_select_fusion.1 = f32[5,512,512]{2,1,0:T(8,128)S(1)} fusion(pred[512,512]{1,0:T(8,128)(4,1)S(1)} %iota_compare_fusion, f32[5,512,112]{1,2,0:T(8,128)S(1)} %bitcast.101, f32[5,512,112]{1,2,0:T(8,128)S(1)} %bitcast.98), kind=kOutput, calls=%fused_computation.1 | convolution fusion | flops 882114560 | bytes 7798784 | tf_op jit(solution)/shard_map/hti,hsi->hts/dot_general | solution.py:11
  10.8 3.7 %fusion.9 = f32[5,512,113]{1,2,0:T(8,128)} fusion(f32[5,512,512]{2,1,0:T(8,128)S(1)} %broadcast_select_fusion.1, f32[5,512,112]{1,2,0:T(8,128)S(1)} %bitcast.106), kind=kOutput, calls=%fused_computation.22 | convolution fusion | flops 888668160 | bytes 7546880 | tf_op jit(solution)/shard_map/hts,hsj->htj/dot_general | solution.py:11
  14.5 0.6 collective-permute-done.3
  15.1 1.6 %collective-permute-start.4 = (f32[5,112,113]{2,1,0:T(8,128)S(1)}, f32[5,112,113]{2,1,0:T(8,128)S(1)}, u32[]{:S(2)}, u32[]{:S(2)}) collective-permute-start(f32[5,112,113]{2,1,0:T(8,128)S(1)} %add.129), channel_id=1, source_target_pairs={{0,8},{4,12},{8,0},{12,4},{16,24},{20,28},{24,16},{28,20},{1,9},{5... | collective-permute-start | bytes 759368 | tf_op jit(solution)/shard_map/ppermute | solution.py:15
  16.7 0.9 broadcast_compare_fusion.1
  17.6 6.1 %collective-permute-done.4 = f32[5,112,113]{2,1,0:T(8,128)S(1)} collective-permute-done((f32[5,112,113]{2,1,0:T(8,128)S(1)}, f32[5,112,113]{2,1,0:T(8,128)S(1)}, u32[]{:S(2)}, u32[]{:S(2)}) %collective-permute-start.4) | collective-permute-done | bytes 253152 | tf_op jit(solution)/shard_map/ppermute | solution.py:15
  23.7 0.8 add.131
  24.6 2.6 %collective-permute-start.5 = (f32[5,112,113]{2,1,0:T(8,128)}, f32[5,112,113]{2,1,0:T(8,128)}, u32[]{:S(2)}, u32[]{:S(2)}) collective-permute-start(f32[5,112,113]{2,1,0:T(8,128)} %add.131), channel_id=1, source_target_pairs={{0,16},{4,20},{8,24},{12,28},{16,0},{20,4},{24,8},{28,12},{1,17},{... | collective-permute-start | bytes 759368 | tf_op jit(solution)/shard_map/ppermute | solution.py:15
  27.2 0.9 broadcast_compare_fusion
  28.0 2.7 %broadcast_in_dim.32 = f32[512,2240]{0,1:T(8,128)} broadcast(f32[]{:T(128)} %constant.77.clone.1), dimensions={} | broadcast | bytes 4587524 | tf_op jit(solution)/shard_map/broadcast_in_dim | solution.py:68
  30.8 1.1 constant_dynamic-update-slice_fusion.3
  31.9 7.8 %collective-permute-done.5 = f32[5,112,113]{2,1,0:T(8,128)} collective-permute-done((f32[5,112,113]{2,1,0:T(8,128)}, f32[5,112,113]{2,1,0:T(8,128)}, u32[]{:S(2)}, u32[]{:S(2)}) %collective-permute-start.5) | collective-permute-done | bytes 253152 | tf_op jit(solution)/shard_map/ppermute | solution.py:15
  39.8 2.0 %convolution_add_fusion = f32[5,512,113]{1,2,0:T(8,128)S(1)} fusion(f32[5,512,113]{1,2,0:T(8,128)} %fusion.9, f32[5,512,112]{1,2,0:T(8,128)S(1)} %bitcast.102, f32[5,112,113]{2,1,0:T(8,128)S(1)} %select_add_fusion.1), kind=kOutput, calls=%fused_computation.2 | convolution fusion | flops 194685440 | bytes 3714240 | tf_op jit(solution)/shard_map/hti,hij->htj/dot_general | solution.py:11
  41.9 0.2 slice_divide_fusion
  42.0 2.4 %constant_dynamic-update-slice_fusion.2 = f32[512,2240]{0,1:T(8,128)} fusion(f32[512,2240]{0,1:T(8,128)} %constant_dynamic-update-slice_fusion.3, f32[512,560]{0,1:T(8,128)} %collective-permute-done, s32[]{:T(128)S(6)} %select_n.115), kind=kLoop, calls=%fused_computation.56 | loop fusion | bytes 2293764 | tf_op jit(solution)/shard_map/dynamic_update_slice | solution.py:70
  44.5 2.4 %constant_dynamic-update-slice_fusion.1 = f32[512,2240]{0,1:T(8,128)} fusion(f32[512,2240]{0,1:T(8,128)} %constant_dynamic-update-slice_fusion.2, f32[512,560]{0,1:T(8,128)} %collective-permute-done.1, s32[]{:T(128)S(6)} %select_n.116), kind=kLoop, calls=%fused_computation.55 | loop fusion | bytes 2293764 | tf_op jit(solution)/shard_map/dynamic_update_slice | solution.py:70
  46.8 1.1 constant_dynamic-update-slice_fusion
  47.9 8.1 %fusion.23 = f32[8,280,560]{2,1,0:T(8,128)S(1)} fusion(f32[512,8,280]{0,2,1:T(8,128)} %bitcast.1, f32[512,560,1]{0,1,2:T(8,128)S(1)} %bitcast.115), kind=kOutput, calls=%fused_computation.66 | convolution fusion | flops 3853516800 | bytes 10752000 | tf_op jit(solution)/shard_map/tgd,tc->gdc/dot_general | solution.py:11
  56.0 0.1 slice.27
  56.1 0.3 fusion.22
  56.5 0.1 dynamic-slice_bitcast_fusion.1
  56.6 1.7 %collective-permute-start.6 = (f32[2,2,56,560]{3,2,1,0:T(8,128)S(1)}, f32[2,2,56,560]{3,2,1,0:T(8,128)S(1)}, u32[]{:S(2)}, u32[]{:S(2)}) collective-permute-start(f32[2,2,56,560]{3,2,1,0:T(8,128)S(1)} %dynamic-slice_bitcast_fusion.4), channel_id=1, source_target_pairs={{0,8},{4,12},{8,0},{12,4},{16,24},{20,28},{24,16},{28,20},{1,9},{5... | collective-permute-start | bytes 1505288 | tf_op jit(solution)/shard_map/ppermute | solution.py:15
  58.3 0.1 dynamic-slice_bitcast_fusion
  58.3 1.6 %collective-permute-start.7 = (f32[2,2,112,560]{3,2,1,0:T(8,128)S(1)}, f32[2,2,112,560]{3,2,1,0:T(8,128)S(1)}, u32[]{:S(2)}, u32[]{:S(2)}) collective-permute-start(f32[2,2,112,560]{3,2,1,0:T(8,128)S(1)} %dynamic-slice_bitcast_fusion.1), channel_id=1, source_target_pairs={{0,4},{4,0},{8,12},{12,8},{16,20},{20,16},{24,28},{28,24},{1,5},{5... | collective-permute-start | bytes 3010568 | tf_op jit(solution)/shard_map/ppermute | solution.py:15
  60.0 7.0 %fusion.24 = f32[512,560]{0,1:T(8,128)S(1)} fusion(f32[512,2240]{0,1:T(8,128)} %constant_dynamic-update-slice_fusion, f32[2240,560]{0,1:T(8,128)S(1)} %bitcast.125), kind=kOutput, calls=%fused_computation.67 | convolution fusion | flops 3853516800 | bytes 10752000 | tf_op jit(solution)/shard_map/dot_general | solution.py:101
  67.0 4.4 %collective-permute-done.6 = f32[2,2,56,560]{3,2,1,0:T(8,128)S(1)} collective-permute-done((f32[2,2,56,560]{3,2,1,0:T(8,128)S(1)}, f32[2,2,56,560]{3,2,1,0:T(8,128)S(1)}, u32[]{:S(2)}, u32[]{:S(2)}) %collective-permute-start.6) | collective-permute-done | bytes 501792 | tf_op jit(solution)/shard_map/ppermute | solution.py:15
  71.4 0.3 broadcast_divide_fusion
  71.7 0.7 fusion.11
  72.5 1.6 %collective-permute-start.8 = (f32[5,112,113]{2,1,0:T(8,128)S(1)}, f32[5,112,113]{2,1,0:T(8,128)S(1)}, u32[]{:S(2)}, u32[]{:S(2)}) collective-permute-start(f32[5,112,113]{2,1,0:T(8,128)S(1)} %fusion.11), channel_id=1, source_target_pairs={{0,4},{4,0},{8,12},{12,8},{16,20},{20,16},{24,28},{28,24},{1,5},{5... | collective-permute-start | bytes 759368 | tf_op jit(solution)/shard_map/ppermute | solution.py:15
  74.2 2.7 %broadcast_select_fusion = f32[5,512,512]{2,1,0:T(8,128)S(1)} fusion(pred[512,512]{1,0:T(8,128)(4,1)S(1)} %copy-done.5, f32[5,512,112]{1,2,0:T(8,128)S(1)} %bitcast.107, f32[5,512,1]{1,2,0:T(1,128)S(1)} %reshape_divide_fusion, f32[5,512,112]{1,2,0:T(8,128)S(1)} %get-tuple-element.24), kind=kOutput, calls=%fused_computation | convolution fusion | flops 890268160 | bytes 7809024 | tf_op jit(solution)/shard_map/htj,hsj->hts/dot_general | solution.py:11
  77.0 0.6 fusion.12
  77.6 13.8 %collective-permute-done.8 = f32[5,112,113]{2,1,0:T(8,128)S(1)} collective-permute-done((f32[5,112,113]{2,1,0:T(8,128)S(1)}, f32[5,112,113]{2,1,0:T(8,128)S(1)}, u32[]{:S(2)}, u32[]{:S(2)}) %collective-permute-start.8) | collective-permute-done | bytes 253152 | tf_op jit(solution)/shard_map/ppermute | solution.py:15
  91.5 0.4 collective-permute-start.9
  91.9 3.5 %collective-permute-start.16 = (f32[2,56,560]{2,1,0:T(8,128)S(1)}, f32[2,56,560]{2,1,0:T(8,128)S(1)}, u32[]{:S(2)}, u32[]{:S(2)}) collective-permute-start(f32[2,56,560]{2,1,0:T(8,128)S(1)} %dynamic-slice_bitcast_fusion.5), channel_id=1, source_target_pairs={{0,16},{4,20},{8,24},{12,28},{16,0},{20,4},{24,8},{28,12},{1,17},{... | collective-permute-start | bytes 752648 | tf_op jit(solution)/shard_map/ppermute | solution.py:15
  95.3 0.2 bitcast_add_fusion.1
  95.5 1.8 %collective-permute-start.11 = (f32[2,112,560]{2,1,0:T(8,128)S(1)}, f32[2,112,560]{2,1,0:T(8,128)S(1)}, u32[]{:S(2)}, u32[]{:S(2)}) collective-permute-start(f32[2,112,560]{2,1,0:T(8,128)S(1)} %dynamic-slice_bitcast_fusion.3), channel_id=1, source_target_pairs={{0,8},{4,12},{8,0},{12,4},{16,24},{20,28},{24,16},{28,20},{1,9},{5... | collective-permute-start | bytes 1505288 | tf_op jit(solution)/shard_map/ppermute | solution.py:15
  97.3 1.5 collective-permute-start.13
  98.9 3.6 %fusion.1 = f32[512,5,112]{0,2,1:T(8,128)} fusion(pred[512,5,112]{0,2,1:T(8,128)(4,1)S(1)} %bitcast.119, f32[5,512,112]{1,2,0:T(8,128)S(1)} %fusion.12, f32[5,512,512]{2,1,0:T(8,128)S(1)} %broadcast_select_fusion, f32[5,512,112]{1,2,0:T(8,128)S(1)} %bitcast.99), kind=kOutput, calls=%fused_computation.7 | convolution fusion | flops 881377280 | bytes 8970240 | tf_op jit(solution)/shard_map/hts,hsi->hti/dot_general | solution.py:11
  102.5 5.6 %collective-permute-done.9 = f32[5,112,113]{2,1,0:T(8,128)S(1)} collective-permute-done((f32[5,112,113]{2,1,0:T(8,128)S(1)}, f32[5,112,113]{2,1,0:T(8,128)S(1)}, u32[]{:S(2)}, u32[]{:S(2)}) %collective-permute-start.9) | collective-permute-done | bytes 253152 | tf_op jit(solution)/shard_map/ppermute | solution.py:15
  108.2 0.1 collective-permute-start.10
  108.3 1.6 %collective-permute-start.17 = (f32[56,560]{1,0:T(8,128)S(1)}, f32[56,560]{1,0:T(8,128)S(1)}, u32[]{:S(2)}, u32[]{:S(2)}) collective-permute-start(f32[56,560]{1,0:T(8,128)S(1)} %dynamic-slice_bitcast_fusion.8), channel_id=1, source_target_pairs={{0,4},{4,0},{8,12},{12,8},{16,20},{20,16},{24,28},{28,24},{1,5},{5... | collective-permute-start | bytes 376328 | tf_op jit(solution)/shard_map/ppermute | solution.py:15
  110.0 11.6 %collective-permute-done.10 = f32[5,112,113]{2,1,0:T(8,128)S(1)} collective-permute-done((f32[5,112,113]{2,1,0:T(8,128)S(1)}, f32[5,112,113]{2,1,0:T(8,128)S(1)}, u32[]{:S(2)}, u32[]{:S(2)}) %collective-permute-start.10) | collective-permute-done | bytes 253152 | tf_op jit(solution)/shard_map/ppermute | solution.py:15
  121.5 0.1 select_add_fusion
  121.6 0.6 fusion.4
  122.3 0.7 fusion.13
  123.0 2.5 %fusion.3 = f32[512,5,112]{0,2,1:T(8,128)} fusion(pred[512,5,112]{0,2,1:T(8,128)(4,1)S(1)} %bitcast.118, f32[5,512,112]{1,2,0:T(8,128)S(1)} %fusion.4, f32[5,512,512]{2,1,0:T(8,128)S(1)} %broadcast_select_fusion, f32[5,512,112]{1,2,0:T(8,128)S(1)} %bitcast.104), kind=kOutput, calls=%fused_computation.9 | convolution fusion | flops 881377280 | bytes 8970240 | tf_op jit(solution)/shard_map/hts,hti->hsi/dot_general | solution.py:11
  125.5 0.2 bitcast_add_fusion
  125.7 5.7 %collective-permute-start.14 = (f32[2,112,560]{2,1,0:T(8,128)S(1)}, f32[2,112,560]{2,1,0:T(8,128)S(1)}, u32[]{:S(2)}, u32[]{:S(2)}) collective-permute-start(f32[2,112,560]{2,1,0:T(8,128)S(1)} %dynamic-slice_bitcast_fusion.2), channel_id=1, source_target_pairs={{0,8},{4,12},{8,0},{12,4},{16,24},{20,28},{24,16},{28,20},{1,9},{5... | collective-permute-start | bytes 1505288 | tf_op jit(solution)/shard_map/ppermute | solution.py:15
  131.4 2.5 %convolution_add_fusion.1 = f32[5,512,112]{1,2,0:T(8,128)} fusion(f32[5,512,112]{1,2,0:T(8,128)S(1)} %fusion.13, f32[5,512,512]{2,1,0:T(8,128)S(1)} %bitcast.96, f32[5,512,112]{1,2,0:T(8,128)S(1)} %get-tuple-element.24), kind=kOutput, calls=%fused_computation.3 | convolution fusion | flops 881090560 | bytes 8683520 | tf_op jit(solution)/shard_map/hts,htj->hsj/dot_general | solution.py:11
  134.0 0.1 bitcast_add_fusion.4
  134.1 0.1 collective-permute-start.12
  134.1 14.5 %collective-permute-done.14 = f32[2,112,560]{2,1,0:T(8,128)S(1)} collective-permute-done((f32[2,112,560]{2,1,0:T(8,128)S(1)}, f32[2,112,560]{2,1,0:T(8,128)S(1)}, u32[]{:S(2)}, u32[]{:S(2)}) %collective-permute-start.14) | collective-permute-done | bytes 501792 | tf_op jit(solution)/shard_map/ppermute | solution.py:15
  148.6 0.1 bitcast_add_fusion.3
  148.7 0.1 collective-permute-start.15
  148.8 0.4 collective-permute-done.12
  149.3 11.5 %collective-permute-done.15 = f32[112,560]{1,0:T(8,128)S(1)} collective-permute-done((f32[112,560]{1,0:T(8,128)S(1)}, f32[112,560]{1,0:T(8,128)S(1)}, u32[]{:S(2)}, u32[]{:S(2)}) %collective-permute-start.15) | collective-permute-done | bytes 250912 | tf_op jit(solution)/shard_map/ppermute | solution.py:15
  160.9 0.9 pad_maximum_fusion.4
  (61 shorter events, 0.7 us)
Async XLA Ops:
  0.6 4.4 %copy-start.1 = (f32[512,560]{0,1:T(8,128)S(1)}, f32[512,560]{0,1:T(8,128)}, u32[]{:S(2)}) copy-start(f32[512,560]{0,1:T(8,128)} %param.7) | copy-start | bytes 3440644
  0.6 31.3 %collective-permute-start.1 = (f32[512,560]{0,1:T(8,128)}, f32[512,560]{0,1:T(8,128)}, u32[]{:S(2)}, u32[]{:S(2)}) collective-permute-start(f32[512,560]{0,1:T(8,128)} %param.9), channel_id=1, source_target_pairs={{0,2},{1,3},{2,0},{3,1},{4,6},{5,7},{6,4},{7,5},{8,10},{9,11},{10,... | collective-permute-start | bytes 3440648 | tf_op jit(solution)/shard_map/ppermute | solution.py:15
  3.7 38.4 %collective-permute-start = (f32[512,560]{0,1:T(8,128)}, f32[512,560]{0,1:T(8,128)}, u32[]{:S(2)}, u32[]{:S(2)}) collective-permute-start(f32[512,560]{0,1:T(8,128)} %param.9), channel_id=1, source_target_pairs={{0,1},{1,0},{2,3},{3,2},{4,5},{5,4},{6,7},{7,6},{8,9},{9,8},{10,11... | collective-permute-start | bytes 3440648 | tf_op jit(solution)/shard_map/ppermute | solution.py:15
  5.1 2.3 %copy-start.2 = (f32[512,560]{0,1:T(8,128)S(1)}, f32[512,560]{0,1:T(8,128)}, u32[]{:S(2)}) copy-start(f32[512,560]{0,1:T(8,128)} %param.5) | copy-start | bytes 3440644
  5.7 9.3 %collective-permute-start.3 = (f32[5,112,113]{2,1,0:T(8,128)S(1)}, f32[5,112,113]{2,1,0:T(8,128)S(1)}, u32[]{:S(2)}, u32[]{:S(2)}) collective-permute-start(f32[5,112,113]{2,1,0:T(8,128)S(1)} %fusion.7), channel_id=1, source_target_pairs={{0,4},{4,0},{8,12},{12,8},{16,20},{20,16},{24,28},{28,24},{1,5},{5... | collective-permute-start | bytes 759368 | tf_op jit(solution)/shard_map/ppermute | solution.py:15
  7.4 0.7 copy-start.4
  10.8 3.7 %copy-start = (f32[5,512,512]{2,1,0:T(8,128)}, f32[5,512,512]{2,1,0:T(8,128)S(1)}, u32[]{:S(2)}) copy-start(f32[5,512,512]{2,1,0:T(8,128)S(1)} %broadcast_select_fusion.1) | copy-start | bytes 15728644
  15.0 9.5 %copy-start.9 = (f32[5,112,113]{2,1,0:T(8,128)}, f32[5,112,113]{2,1,0:T(8,128)S(1)}, u32[]{:S(2)}) copy-start(f32[5,112,113]{2,1,0:T(8,128)S(1)} %collective-permute-done.3) | copy-start | bytes 759364
  15.1 12.1 %copy-start.3 = (f32[512,560]{0,1:T(8,128)S(1)}, f32[512,560]{0,1:T(8,128)}, u32[]{:S(2)}) copy-start(f32[512,560]{0,1:T(8,128)} %param.6) | copy-start | bytes 3440644
  15.1 8.6 %collective-permute-start.4 = (f32[5,112,113]{2,1,0:T(8,128)S(1)}, f32[5,112,113]{2,1,0:T(8,128)S(1)}, u32[]{:S(2)}, u32[]{:S(2)}) collective-permute-start(f32[5,112,113]{2,1,0:T(8,128)S(1)} %add.129), channel_id=1, source_target_pairs={{0,8},{4,12},{8,0},{12,4},{16,24},{20,28},{24,16},{28,20},{1,9},{5... | collective-permute-start | bytes 759368 | tf_op jit(solution)/shard_map/ppermute | solution.py:15
  23.7 4.3 %copy-start.10 = (f32[5,112,113]{2,1,0:T(8,128)}, f32[5,112,113]{2,1,0:T(8,128)S(1)}, u32[]{:S(2)}) copy-start(f32[5,112,113]{2,1,0:T(8,128)S(1)} %collective-permute-done.4) | copy-start | bytes 759364
  24.6 15.2 %collective-permute-start.5 = (f32[5,112,113]{2,1,0:T(8,128)}, f32[5,112,113]{2,1,0:T(8,128)}, u32[]{:S(2)}, u32[]{:S(2)}) collective-permute-start(f32[5,112,113]{2,1,0:T(8,128)} %add.131), channel_id=1, source_target_pairs={{0,16},{4,20},{8,24},{12,28},{16,0},{20,4},{24,8},{28,12},{1,17},{... | collective-permute-start | bytes 759368 | tf_op jit(solution)/shard_map/ppermute | solution.py:15
  28.0 2.7 %copy-start.6 = (f32[512,560]{0,1:T(8,128)S(1)}, f32[512,560]{0,1:T(8,128)}, u32[]{:S(2)}) copy-start(f32[512,560]{0,1:T(8,128)} %param.9) | copy-start | bytes 3440644
  31.9 14.9 %collective-permute-start.2 = (f32[512,560]{0,1:T(8,128)}, f32[512,560]{0,1:T(8,128)S(1)}, u32[]{:S(2)}, u32[]{:S(2)}) collective-permute-start(f32[512,560]{0,1:T(8,128)} %collective-permute-done.1), channel_id=1, source_target_pairs={{0,1},{1,0},{2,3},{3,2},{4,5},{5,4},{6,7},{7,6},{8,9},{9,8},{10,11... | collective-permute-start | bytes 3440648 | tf_op jit(solution)/shard_map/ppermute | solution.py:15
  56.0 4.0 %slice-start.2 = ((s8[5160960]{0:T(1024)(128)(4,1)}), s8[4194304]{0:T(1024)(128)(4,1)S(1)}, s32[]{:S(2)}) async-start(s8[5160960]{0:T(1024)(128)(4,1)} %bitcast.124), calls=%async_computation.2 | async-start | bytes 8388608
  56.1 3.9 %slice-start.3 = ((s8[5160960]{0:T(1024)(128)(4,1)}), s8[966656]{0:T(1024)(128)(4,1)S(1)}, s32[]{:S(2)}) async-start(s8[5160960]{0:T(1024)(128)(4,1)} %bitcast.124), calls=%async_computation.3 | async-start | bytes 1933312
  56.6 14.8 %collective-permute-start.6 = (f32[2,2,56,560]{3,2,1,0:T(8,128)S(1)}, f32[2,2,56,560]{3,2,1,0:T(8,128)S(1)}, u32[]{:S(2)}, u32[]{:S(2)}) collective-permute-start(f32[2,2,56,560]{3,2,1,0:T(8,128)S(1)} %dynamic-slice_bitcast_fusion.4), channel_id=1, source_target_pairs={{0,8},{4,12},{8,0},{12,4},{16,24},{20,28},{24,16},{28,20},{1,9},{5... | collective-permute-start | bytes 1505288 | tf_op jit(solution)/shard_map/ppermute | solution.py:15
  58.3 33.5 %collective-permute-start.7 = (f32[2,2,112,560]{3,2,1,0:T(8,128)S(1)}, f32[2,2,112,560]{3,2,1,0:T(8,128)S(1)}, u32[]{:S(2)}, u32[]{:S(2)}) collective-permute-start(f32[2,2,112,560]{3,2,1,0:T(8,128)S(1)} %dynamic-slice_bitcast_fusion.1), channel_id=1, source_target_pairs={{0,4},{4,0},{8,12},{12,8},{16,20},{20,16},{24,28},{28,24},{1,5},{5... | collective-permute-start | bytes 3010568 | tf_op jit(solution)/shard_map/ppermute | solution.py:15
  72.5 1.7 %copy-start.5 = (pred[512,512]{1,0:T(8,128)(4,1)S(1)}, pred[512,512]{1,0:T(8,128)(4,1)}, u32[]{:S(2)}) copy-start(pred[512,512]{1,0:T(8,128)(4,1)} %copy-done.4) | copy-start | bytes 786436
  72.5 18.9 %collective-permute-start.8 = (f32[5,112,113]{2,1,0:T(8,128)S(1)}, f32[5,112,113]{2,1,0:T(8,128)S(1)}, u32[]{:S(2)}, u32[]{:S(2)}) collective-permute-start(f32[5,112,113]{2,1,0:T(8,128)S(1)} %fusion.11), channel_id=1, source_target_pairs={{0,4},{4,0},{8,12},{12,8},{16,20},{20,16},{24,28},{28,24},{1,5},{5... | collective-permute-start | bytes 759368 | tf_op jit(solution)/shard_map/ppermute | solution.py:15
  91.5 16.6 %collective-permute-start.9 = (f32[5,112,113]{2,1,0:T(8,128)S(1)}, f32[5,112,113]{2,1,0:T(8,128)S(1)}, u32[]{:S(2)}, u32[]{:S(2)}) collective-permute-start(f32[5,112,113]{2,1,0:T(8,128)S(1)} %add.139), channel_id=1, source_target_pairs={{0,8},{4,12},{8,0},{12,4},{16,24},{20,28},{24,16},{28,20},{1,9},{5... | collective-permute-start | bytes 759368 | tf_op jit(solution)/shard_map/ppermute | solution.py:15
  91.9 16.4 %collective-permute-start.16 = (f32[2,56,560]{2,1,0:T(8,128)S(1)}, f32[2,56,560]{2,1,0:T(8,128)S(1)}, u32[]{:S(2)}, u32[]{:S(2)}) collective-permute-start(f32[2,56,560]{2,1,0:T(8,128)S(1)} %dynamic-slice_bitcast_fusion.5), channel_id=1, source_target_pairs={{0,16},{4,20},{8,24},{12,28},{16,0},{20,4},{24,8},{28,12},{1,17},{... | collective-permute-start | bytes 752648 | tf_op jit(solution)/shard_map/ppermute | solution.py:15
  95.5 3.4 %copy-start.8 = (pred[512,560]{0,1:T(8,128)(4,1)S(1)}, pred[512,560]{0,1:T(8,128)(4,1)}, u32[]{:S(2)}) copy-start(pred[512,560]{0,1:T(8,128)(4,1)} %broadcast_compare_fusion.1) | copy-start | bytes 860164
  95.5 38.4 %collective-permute-start.11 = (f32[2,112,560]{2,1,0:T(8,128)S(1)}, f32[2,112,560]{2,1,0:T(8,128)S(1)}, u32[]{:S(2)}, u32[]{:S(2)}) collective-permute-start(f32[2,112,560]{2,1,0:T(8,128)S(1)} %dynamic-slice_bitcast_fusion.3), channel_id=1, source_target_pairs={{0,8},{4,12},{8,0},{12,4},{16,24},{20,28},{24,16},{28,20},{1,9},{5... | collective-permute-start | bytes 1505288 | tf_op jit(solution)/shard_map/ppermute | solution.py:15
  97.3 28.2 %collective-permute-start.13 = (f32[2,2,112,560]{3,2,1,0:T(8,128)S(1)}, f32[2,2,112,560]{3,2,1,0:T(8,128)S(1)}, u32[]{:S(2)}, u32[]{:S(2)}) collective-permute-start(f32[2,2,112,560]{3,2,1,0:T(8,128)S(1)} %dynamic-slice_bitcast_fusion), channel_id=1, source_target_pairs={{0,4},{4,0},{8,12},{12,8},{16,20},{20,16},{24,28},{28,24},{1,5},{5... | collective-permute-start | bytes 3010568 | tf_op jit(solution)/shard_map/ppermute | solution.py:15
  108.2 13.4 %collective-permute-start.10 = (f32[5,112,113]{2,1,0:T(8,128)S(1)}, f32[5,112,113]{2,1,0:T(8,128)S(1)}, u32[]{:S(2)}, u32[]{:S(2)}) collective-permute-start(f32[5,112,113]{2,1,0:T(8,128)S(1)} %add.141), channel_id=1, source_target_pairs={{0,16},{4,20},{8,24},{12,28},{16,0},{20,4},{24,8},{28,12},{1,17},{... | collective-permute-start | bytes 759368 | tf_op jit(solution)/shard_map/ppermute | solution.py:15
  108.3 40.5 %collective-permute-start.17 = (f32[56,560]{1,0:T(8,128)S(1)}, f32[56,560]{1,0:T(8,128)S(1)}, u32[]{:S(2)}, u32[]{:S(2)}) collective-permute-start(f32[56,560]{1,0:T(8,128)S(1)} %dynamic-slice_bitcast_fusion.8), channel_id=1, source_target_pairs={{0,4},{4,0},{8,12},{12,8},{16,20},{20,16},{24,28},{28,24},{1,5},{5... | collective-permute-start | bytes 376328 | tf_op jit(solution)/shard_map/ppermute | solution.py:15
  121.6 1.3 copy-start.7
  122.3 9.2 %slice-start = ((s8[5242880]{0:T(1024)(128)(4,1)}), s8[4194304]{0:T(1024)(128)(4,1)S(1)}, s32[]{:S(2)}) async-start(s8[5242880]{0:T(1024)(128)(4,1)} %bitcast.95), calls=%async_computation | async-start | bytes 8388608
  123.0 8.5 %slice-start.1 = ((s8[5242880]{0:T(1024)(128)(4,1)}), s8[1048576]{0:T(1024)(128)(4,1)S(1)}, s32[]{:S(2)}) async-start(s8[5242880]{0:T(1024)(128)(4,1)} %bitcast.95), calls=%async_computation.1 | async-start | bytes 2097152
  125.7 22.9 %collective-permute-start.14 = (f32[2,112,560]{2,1,0:T(8,128)S(1)}, f32[2,112,560]{2,1,0:T(8,128)S(1)}, u32[]{:S(2)}, u32[]{:S(2)}) collective-permute-start(f32[2,112,560]{2,1,0:T(8,128)S(1)} %dynamic-slice_bitcast_fusion.2), channel_id=1, source_target_pairs={{0,8},{4,12},{8,0},{12,4},{16,24},{20,28},{24,16},{28,20},{1,9},{5... | collective-permute-start | bytes 1505288 | tf_op jit(solution)/shard_map/ppermute | solution.py:15
  134.1 15.2 %collective-permute-start.12 = (f32[112,560]{1,0:T(8,128)S(1)}, f32[112,560]{1,0:T(8,128)S(1)}, u32[]{:S(2)}, u32[]{:S(2)}) collective-permute-start(f32[112,560]{1,0:T(8,128)S(1)} %dynamic-slice_bitcast_fusion.7), channel_id=1, source_target_pairs={{0,16},{4,20},{8,24},{12,28},{16,0},{20,4},{24,8},{28,12},{1,17},{... | collective-permute-start | bytes 752648 | tf_op jit(solution)/shard_map/ppermute | solution.py:15
  148.7 12.1 %collective-permute-start.15 = (f32[112,560]{1,0:T(8,128)S(1)}, f32[112,560]{1,0:T(8,128)S(1)}, u32[]{:S(2)}, u32[]{:S(2)}) collective-permute-start(f32[112,560]{1,0:T(8,128)S(1)} %dynamic-slice_bitcast_fusion.6), channel_id=1, source_target_pairs={{0,16},{4,20},{8,24},{12,28},{16,0},{20,4},{24,8},{28,12},{1,17},{... | collective-permute-start | bytes 752648 | tf_op jit(solution)/shard_map/ppermute | solution.py:15

commit v2 on v1

--- a/solution.py
+++ b/solution.py
@@ -85,7 +85,8 @@
     terms = ein("tgd,tc->gdc", whole_grad.reshape(rows, tm, -1), flat)
     share = groups * width // tm
     bits = tm.bit_length() - 1
-    cut = share * 2 // 40 * 8
+    cut = share * 3 // 7 // 8 * 8
+    last = share * 27 // 35 // 8 * 8
     up = list(range(bits))
     around = up[1:] + up[:1]
     left = up[::-1]
@@ -94,21 +95,23 @@
         return terms[:, low:high].reshape((2,) * bits + (high - low, width))
 
     away_a, kept_a, left_a = split(cube_of(0, cut), left, up[0])
-    away_c, kept_c, left_c = split(cube_of(2 * cut, share), left, around[0])
+    away_c, kept_c, left_c = split(cube_of(last, share), left, around[0])
     away_a, away_c, whole_late = lax.optimization_barrier((away_a, away_c, whole_grad))
     arrived_a = exchange(away_a, "tm", 1 << up[0])
     arrived_c = exchange(away_c, "tm", 1 << around[0])
     grad_att = jnp.dot(whole_late, out_weight, precision=HIGH, preferred_element_type=jnp.float32)
     grad_att, arrived_c = lax.optimization_barrier((grad_att, arrived_c))
-    part_b = finish(cube_of(cut, 2 * cut), left, up, arrived_a)
+    part_b = finish(cube_of(cut, last), left, up, arrived_a)
     part_a = finish(kept_a + arrived_a, left_a, up[1:], None)
-    part_c = finish(kept_c + arrived_c, left_c, around[1:], arrived_a)
+    part_c = finish(kept_c + arrived_c, left_c, around[1:], None)
     grad_weight = jnp.concatenate([part_a, part_b, part_c], axis=0)
     grad_att = grad_att.reshape(shape_heads).transpose(1, 0, 2)
     grad_num = grad_att / denom
     grad_den = -jnp.sum(grad_att * attended, axis=2, keepdims=True) / denom
     grad_one = jnp.concatenate([grad_num, grad_den], axis=2)
-    back = scan_others(ein("hti,htj->hij", feat_q, grad_one), "tm", True)
+    local_back = ein("hti,htj->hij", feat_q, grad_one)
+    local_back, _ = lax.optimization_barrier((local_back, arrived_a))
+    back = scan_others(local_back, "tm", True)
     grad_scores = jnp.where(mask, ein("htj,hsj->hts", grad_one, value_one), 0.0)
     grad_scores, scores, _ = lax.optimization_barrier((grad_scores, scores, arrived_a))
     grad_fq = ein("hts,hsi->hti", grad_scores, feat_k) + ein("htj,hij->hti", grad_one, state)

time: 162 us -> 186 us (1.15)
  local copies, waits for them, and re-layouts: 11.2 us -> 31.2 us
  other arithmetic: 6.38 us -> 11.2 us
  matrix products: 38.2 us -> 42.1 us
  starting transfers between devices: 28.5 us -> 26 us
  waiting for transfers between devices: 76.4 us -> 74.4 us
    dynamic_slice x0 -> x9, local copies, waits for them, and re-layouts: none -> 9.94 us  [the longest x6 5.34 us: split(): kept = lax.dynamic_index_in_dim(cube, mine, dim, False)]
    squeeze x9 -> x6, local copies, waits for them, and re-layouts: 0.4 us -> 5.13 us  [split(): away = lax.dynamic_index_in_dim(cube, 1 - mine, dim, False)]
    unnamed x31 -> x54, local copies, waits for them, and re-layouts: 0.66 us -> 3.69 us
    dot_general x13, matrix products: 31.2 us -> 34.2 us  [ein(): jnp.einsum(spec, a, b, precision=HIGH, preferred_element_type=jnp.float32)]
    add x7, other arithmetic: 0.41 us -> 3.11 us  [finish(): cube = kept + exchange(away, 'tm', 1 << bit)]
    ppermute x18, starting transfers between devices: 28.5 us -> 26 us  [exchange(): lax.ppermute(a, axis, [(i, i ^ bit) for i in range(lax.axis_size(axis))])]
    slice x2 -> x3, local copies, waits for them, and re-layouts: 0.37 us -> 2.77 us  [cube_of(): return terms[:, low:high].reshape((2,) * bits + (high - low, width))]
    ppermute x18, waiting for transfers between devices: 76.4 us -> 74.4 us  [exchange(): lax.ppermute(a, axis, [(i, i ^ bit) for i in range(lax.axis_size(axis))])]
  transfers between devices with their start and end apart: 18 -> 18, of which waited for: 10 -> 11; matrix products, arithmetic and copies ran while one was open for 28% -> 34% of each run, Pallas kernels for 0% -> 0%
where the time goes in v2:
time: 186 us
  waiting for transfers between devices  74.4 us (40%)
  matrix products  42.1 us (23%)
  local copies, waits for them, and re-layouts  31.2 us (17%)
  starting transfers between devices  26 us (14%)
  other arithmetic  11.2 us (6%)
    ppermute x18, waiting for transfers between devices, exchange(): lax.ppermute(a, axis, [(i, i ^ bit) for i in range(lax.axis_size(axis))])  74.4 us
    dot_general x13, matrix products, ein(): jnp.einsum(spec, a, b, precision=HIGH, preferred_element_type=jnp.float32)  34.2 us
    ppermute x18, starting transfers between devices, exchange(): lax.ppermute(a, axis, [(i, i ^ bit) for i in range(lax.axis_size(axis))])  26 us
    dot_general x1, matrix products, shards(): jnp.dot(whole_late, out_weight, precision=HIGH, preferred_element_type=jn...  7.92 us
    dynamic_update_slice x4, local copies, waits for them, and re-layouts, shards(): lax.dynamic_update_slice_in_dim(whole_grad, block, (head ^ k) * width, 1)  6.95 us
    dynamic_slice x6, local copies, waits for them, and re-layouts, split(): kept = lax.dynamic_index_in_dim(cube, mine, dim, False)  5.34 us
    squeeze x6, local copies, waits for them, and re-layouts, split(): away = lax.dynamic_index_in_dim(cube, 1 - mine, dim, False)  5.13 us
    dynamic_slice x3, local copies, waits for them, and re-layouts, split(): away = lax.dynamic_index_in_dim(cube, 1 - mine, dim, False)  4.61 us
  transfers between devices with their start and end apart: 18, of which 11 were waited for; matrix products, arithmetic and copies ran while one was open for 34% of the time, Pallas kernels for 0%

profile of v2, /device:TPU:0, one launch (start us, length us, event | category | flops | bytes accessed | tf_op | source)
XLA Modules:
  0.0 185.9 jit_solution(1050100622127931335)
XLA Ops:
  1.2 2.6 %collective-permute-start.1 = (f32[512,560]{0,1:T(8,128)}, f32[512,560]{0,1:T(8,128)}, u32[]{:S(2)}, u32[]{:S(2)}) collective-permute-start(f32[512,560]{0,1:T(8,128)} %param.9), channel_id=1, source_target_pairs={{0,2},{1,3},{2,0},{3,1},{4,6},{5,7},{6,4},{7,5},{8,10},{9,11},{10,... | collective-permute-start | bytes 3440648 | tf_op jit(solution)/shard_map/ppermute | solution.py:15
  3.8 1.4 broadcast_maximum_fusion
  5.2 0.7 fusion.7
  5.9 1.6 collective-permute-start.3
  8.2 2.7 %broadcast_select_fusion.1 = f32[5,512,512]{2,1,0:T(8,128)S(1)} fusion(pred[512,512]{1,0:T(8,128)(4,1)S(1)} %iota_compare_fusion, f32[5,512,112]{1,2,0:T(8,128)S(1)} %bitcast.102, f32[5,512,112]{1,2,0:T(8,128)S(1)} %bitcast.99), kind=kOutput, calls=%fused_computation.1 | convolution fusion | flops 882114560 | bytes 7798784 | tf_op jit(solution)/shard_map/hti,hsi->hts/dot_general | solution.py:11
  10.9 2.7 %fusion.9 = f32[5,512,113]{1,2,0:T(8,128)S(1)} fusion(f32[5,512,512]{2,1,0:T(8,128)S(1)} %broadcast_select_fusion.1, f32[5,512,112]{1,2,0:T(8,128)S(1)} %bitcast.107), kind=kOutput, calls=%fused_computation.19 | convolution fusion | flops 888668160 | bytes 7546880 | tf_op jit(solution)/shard_map/hts,hsj->htj/dot_general | solution.py:11
  13.6 1.2 collective-permute-done.3
  14.9 1.6 collective-permute-start.4
  16.5 0.9 broadcast_compare_fusion
  17.4 5.7 %collective-permute-done.4 = f32[5,112,113]{2,1,0:T(8,128)S(1)} collective-permute-done((f32[5,112,113]{2,1,0:T(8,128)S(1)}, f32[5,112,113]{2,1,0:T(8,128)S(1)}, u32[]{:S(2)}, u32[]{:S(2)}) %collective-permute-start.4) | collective-permute-done | bytes 253152 | tf_op jit(solution)/shard_map/ppermute | solution.py:15
  23.1 0.8 add.134
  23.9 2.6 %collective-permute-start.5 = (f32[5,112,113]{2,1,0:T(8,128)}, f32[5,112,113]{2,1,0:T(8,128)}, u32[]{:S(2)}, u32[]{:S(2)}) collective-permute-start(f32[5,112,113]{2,1,0:T(8,128)} %add.134), channel_id=1, source_target_pairs={{0,16},{4,20},{8,24},{12,28},{16,0},{20,4},{24,8},{28,12},{1,17},{... | collective-permute-start | bytes 759368 | tf_op jit(solution)/shard_map/ppermute | solution.py:15
  26.5 0.9 broadcast_compare_fusion.1
  27.4 2.7 %broadcast_in_dim.32 = f32[512,2240]{0,1:T(8,128)} broadcast(f32[]{:T(128)} %constant.83.clone.1), dimensions={} | broadcast | bytes 4587524 | tf_op jit(solution)/shard_map/broadcast_in_dim | solution.py:68
  30.1 1.1 constant_dynamic-update-slice_fusion.3
  31.2 7.4 %collective-permute-done.5 = f32[5,112,113]{2,1,0:T(8,128)} collective-permute-done((f32[5,112,113]{2,1,0:T(8,128)}, f32[5,112,113]{2,1,0:T(8,128)}, u32[]{:S(2)}, u32[]{:S(2)}) %collective-permute-start.5) | collective-permute-done | bytes 253152 | tf_op jit(solution)/shard_map/ppermute | solution.py:15
  38.7 0.7 convolution_add_fusion
  39.7 0.9 copy-done.5
  40.5 2.3 %constant_dynamic-update-slice_fusion.2 = f32[512,2240]{0,1:T(8,128)} fusion(f32[512,2240]{0,1:T(8,128)} %constant_dynamic-update-slice_fusion.3, f32[512,560]{0,1:T(8,128)} %collective-permute-done, s32[]{:T(128)S(6)} %select_n.118), kind=kLoop, calls=%fused_computation.59 | loop fusion | bytes 2293764 | tf_op jit(solution)/shard_map/dynamic_update_slice | solution.py:70
  42.9 2.4 %constant_dynamic-update-slice_fusion.1 = f32[512,2240]{0,1:T(8,128)} fusion(f32[512,2240]{0,1:T(8,128)} %constant_dynamic-update-slice_fusion.2, f32[512,560]{0,1:T(8,128)} %collective-permute-done.1, s32[]{:T(128)S(6)} %select_n.119), kind=kLoop, calls=%fused_computation.58 | loop fusion | bytes 2293764 | tf_op jit(solution)/shard_map/dynamic_update_slice | solution.py:70
  45.3 1.1 constant_dynamic-update-slice_fusion
  46.4 8.1 %fusion.22 = f32[8,280,560]{2,1,0:T(8,128)S(1)} fusion(f32[512,8,280]{0,2,1:T(8,128)} %bitcast.1, f32[512,560,1]{0,1,2:T(8,128)S(1)} %bitcast.115), kind=kOutput, calls=%fused_computation.68 | convolution fusion | flops 3853516800 | bytes 10752000 | tf_op jit(solution)/shard_map/tgd,tc->gdc/dot_general | solution.py:11
  54.6 1.1 slice.27
  55.8 1.5 slice.29
  57.2 1.2 constant_dynamic-slice_fusion.4
  58.5 2.7 %copy.29 = f32[2,2,1,120,560]{3,4,1,0,2:T(8,128)} copy(f32[2,2,1,120,560]{4,3,2,1,0:T(8,128)} %get-tuple-element.35) | data formatting | bytes 2150400 | tf_op jit(solution)/shard_map/jit(dynamic_index_in_dim)/dynamic_slice | solution.py:45
  61.1 2.0 %dynamic-slice_bitcast_fusion.1 = f32[2,2,64,560]{3,2,1,0:T(8,128)} fusion(f32[2,2,2,64,560]{4,3,2,1,0:T(8,128)} %bitcast.113, s32[]{:T(128)S(6)} %select_n.131), kind=kLoop, calls=%fused_computation.28 | loop fusion | bytes 1146884 | tf_op jit(solution)/shard_map/jit(dynamic_index_in_dim)/squeeze | solution.py:45
  63.1 2.4 %collective-permute-start.7 = (f32[2,2,120,560]{2,3,1,0:T(8,128)}, f32[2,2,120,560]{2,3,1,0:T(8,128)}, u32[]{:S(2)}, u32[]{:S(2)}) collective-permute-start(f32[2,2,120,560]{2,3,1,0:T(8,128)} %bitcast.14), channel_id=1, source_target_pairs={{0,4},{4,0},{8,12},{12,8},{16,20},{20,16},{24,28},{28,24},{1,5},{5... | collective-permute-start | bytes 3225608 | tf_op jit(solution)/shard_map/ppermute | solution.py:15
  65.5 1.4 copy.31
  66.9 2.3 %dynamic-slice_bitcast_fusion = f32[2,2,96,560]{3,2,1,0:T(8,128)} fusion(f32[2,2,2,96,560]{4,3,2,1,0:T(8,128)} %bitcast.111, s32[]{:T(128)S(6)} %select_n.129), kind=kLoop, calls=%fused_computation.23 | loop fusion | bytes 1720324 | tf_op jit(solution)/shard_map/jit(dynamic_index_in_dim)/squeeze | solution.py:45
  69.2 0.8 collective-permute-start.6
  70.0 7.9 %fusion.23 = f32[512,560]{0,1:T(8,128)S(1)} fusion(f32[512,2240]{0,1:T(8,128)} %constant_dynamic-update-slice_fusion, f32[2240,560]{0,1:T(8,128)} %param.8), kind=kOutput, calls=%fused_computation.69 | convolution fusion | flops 3853516800 | bytes 10752000 | tf_op jit(solution)/shard_map/dot_general | solution.py:102
  77.9 6.7 %collective-permute-done.6 = f32[2,2,64,560]{3,2,1,0:T(8,128)S(1)} collective-permute-done((f32[2,2,64,560]{3,2,1,0:T(8,128)S(1)}, f32[2,2,64,560]{3,2,1,0:T(8,128)S(1)}, u32[]{:S(2)}, u32[]{:S(2)}) %collective-permute-start.6) | collective-permute-done | bytes 573472 | tf_op jit(solution)/shard_map/ppermute | solution.py:15
  84.7 3.5 %collective-permute-start.16 = (f32[2,64,560]{2,1,0:T(8,128)S(1)}, f32[2,64,560]{2,1,0:T(8,128)S(1)}, u32[]{:S(2)}, u32[]{:S(2)}) collective-permute-start(f32[2,64,560]{2,1,0:T(8,128)S(1)} %dynamic-slice_bitcast_fusion.4), channel_id=1, source_target_pairs={{0,16},{4,20},{8,24},{12,28},{16,0},{20,4},{24,8},{28,12},{1,17},{... | collective-permute-start | bytes 860168 | tf_op jit(solution)/shard_map/ppermute | solution.py:15
  88.6 0.9 copy-done.3
  89.6 5.0 %broadcast_select_fusion = f32[5,512,512]{2,1,0:T(8,128)} fusion(pred[512,512]{1,0:T(8,128)(4,1)S(1)} %copy-done.14, f32[5,512,112]{1,2,0:T(8,128)S(1)} %bitcast.108, f32[5,512,1]{1,2,0:T(1,128)S(1)} %reshape_divide_fusion, f32[5,512,112]{1,2,0:T(8,128)S(1)} %get-tuple-element.36), kind=kOutput, calls=%fused_computation | convolution fusion | flops 890268160 | bytes 7809024 | tf_op jit(solution)/shard_map/htj,hsj->hts/dot_general | solution.py:11
  94.6 1.4 fusion.11
  95.9 1.6 fusion.12
  97.6 4.9 %collective-permute-done.16 = f32[2,64,560]{2,1,0:T(8,128)S(1)} collective-permute-done((f32[2,64,560]{2,1,0:T(8,128)S(1)}, f32[2,64,560]{2,1,0:T(8,128)S(1)}, u32[]{:S(2)}, u32[]{:S(2)}) %collective-permute-start.16) | collective-permute-done | bytes 286752 | tf_op jit(solution)/shard_map/ppermute | solution.py:15
  102.5 0.8 constant_dynamic-slice_fusion.1
  103.3 1.8 copy.37
  105.5 1.8 copy.36
  107.3 1.5 collective-permute-start.8
  108.8 1.9 %bitcast_add_fusion = f32[2,2,120,560]{2,3,1,0:T(8,128)S(1)} fusion(f32[2,2,120,560]{2,3,1,0:T(8,128)} %collective-permute-done.7, f32[2,2,1,120,560]{3,4,1,0,2:T(8,128)} %copy.31), kind=kLoop, calls=%fused_computation.12 | loop fusion | flops 268800 | bytes 3225600 | tf_op jit(solution)/shard_map/add | solution.py:105
  110.8 0.7 collective-permute-start.11
  111.5 3.6 %collective-permute-done.17 = f32[64,560]{0,1:T(8,128)} collective-permute-done((f32[64,560]{0,1:T(8,128)}, f32[64,560]{0,1:T(8,128)}, u32[]{:S(2)}, u32[]{:S(2)}) %collective-permute-start.17) | collective-permute-done | bytes 143392 | tf_op jit(solution)/shard_map/ppermute | solution.py:15
  115.1 1.8 bitcast_add_fusion.6
  117.4 3.8 %collective-permute-done.8 = f32[5,112,113]{2,1,0:T(8,128)S(1)} collective-permute-done((f32[5,112,113]{2,1,0:T(8,128)}, f32[5,112,113]{2,1,0:T(8,128)S(1)}, u32[]{:S(2)}, u32[]{:S(2)}) %collective-permute-start.8) | collective-permute-done | bytes 253152 | tf_op jit(solution)/shard_map/ppermute | solution.py:15
  121.2 1.0 add.142
  122.2 0.7 collective-permute-start.9
  122.8 4.9 %fusion.1 = f32[512,5,112]{0,2,1:T(8,128)} fusion(pred[512,5,112]{0,2,1:T(8,128)(4,1)S(1)} %bitcast.119, f32[5,512,112]{1,2,0:T(8,128)} %fusion.12, f32[5,512,512]{2,1,0:T(8,128)S(1)} %copy-done, f32[5,512,112]{1,2,0:T(8,128)S(1)} %bitcast.100), kind=kOutput, calls=%fused_computation.7 | convolution fusion | flops 881377280 | bytes 8970240 | tf_op jit(solution)/shard_map/hts,hsi->hti/dot_general | solution.py:11
  127.7 2.7 %collective-permute-done.9 = f32[5,112,113]{2,1,0:T(8,128)S(1)} collective-permute-done((f32[5,112,113]{2,1,0:T(8,128)S(1)}, f32[5,112,113]{2,1,0:T(8,128)S(1)}, u32[]{:S(2)}, u32[]{:S(2)}) %collective-permute-start.9) | collective-permute-done | bytes 253152 | tf_op jit(solution)/shard_map/ppermute | solution.py:15
  130.4 3.3 %collective-permute-start.10 = (f32[5,112,113]{2,1,0:T(8,128)S(1)}, f32[5,112,113]{2,1,0:T(8,128)S(1)}, u32[]{:S(2)}, u32[]{:S(2)}) collective-permute-start(f32[5,112,113]{2,1,0:T(8,128)S(1)} %add.144), channel_id=1, source_target_pairs={{0,16},{4,20},{8,24},{12,28},{16,0},{20,4},{24,8},{28,12},{1,17},{... | collective-permute-start | bytes 759368 | tf_op jit(solution)/shard_map/ppermute | solution.py:15
  133.8 0.8 dynamic-slice_bitcast_fusion.5
  134.6 18.2 %collective-permute-done.10 = f32[5,112,113]{2,1,0:T(8,128)S(1)} collective-permute-done((f32[5,112,113]{2,1,0:T(8,128)S(1)}, f32[5,112,113]{2,1,0:T(8,128)S(1)}, u32[]{:S(2)}, u32[]{:S(2)}) %collective-permute-start.10) | collective-permute-done | bytes 253152 | tf_op jit(solution)/shard_map/ppermute | solution.py:15
  152.9 0.6 fusion.4
  153.6 0.7 fusion.13
  154.3 2.6 %fusion.3 = f32[512,5,112]{0,2,1:T(8,128)} fusion(pred[512,5,112]{0,2,1:T(8,128)(4,1)S(1)} %bitcast.118, f32[5,512,112]{1,2,0:T(8,128)S(1)} %fusion.4, f32[5,512,512]{2,1,0:T(8,128)S(1)} %copy-done, f32[5,512,112]{1,2,0:T(8,128)S(1)} %bitcast.105), kind=kOutput, calls=%fused_computation.9 | convolution fusion | flops 881377280 | bytes 8970240 | tf_op jit(solution)/shard_map/hts,hti->hsi/dot_general | solution.py:11
  157.1 2.5 %convolution_add_fusion.1 = f32[5,512,112]{1,2,0:T(8,128)} fusion(f32[5,512,112]{1,2,0:T(8,128)S(1)} %fusion.13, f32[5,512,512]{2,1,0:T(8,128)S(1)} %bitcast.97, f32[5,512,112]{1,2,0:T(8,128)S(1)} %get-tuple-element.36), kind=kOutput, calls=%fused_computation.3 | convolution fusion | flops 881090560 | bytes 8683520 | tf_op jit(solution)/shard_map/hts,htj->hsj/dot_general | solution.py:11
  159.7 8.8 %collective-permute-done.14 = f32[2,96,560]{2,1,0:T(8,128)S(1)} collective-permute-done((f32[2,96,560]{2,1,0:T(8,128)S(1)}, f32[2,96,560]{2,1,0:T(8,128)S(1)}, u32[]{:S(2)}, u32[]{:S(2)}) %collective-permute-start.14) | collective-permute-done | bytes 430112 | tf_op jit(solution)/shard_map/ppermute | solution.py:15
  168.7 3.1 %collective-permute-start.15 = (f32[96,560]{0,1:T(8,128)S(1)}, f32[96,560]{0,1:T(8,128)S(1)}, u32[]{:S(2)}, u32[]{:S(2)}) collective-permute-start(f32[96,560]{0,1:T(8,128)S(1)} %bitcast.123), channel_id=1, source_target_pairs={{0,16},{4,20},{8,24},{12,28},{16,0},{20,4},{24,8},{28,12},{1,17},{... | collective-permute-start | bytes 645128 | tf_op jit(solution)/shard_map/ppermute | solution.py:15
  171.9 1.0 bitcast_add_fusion.8
  173.0 11.3 %collective-permute-done.15 = f32[96,560]{0,1:T(8,128)S(1)} collective-permute-done((f32[96,560]{0,1:T(8,128)S(1)}, f32[96,560]{0,1:T(8,128)S(1)}, u32[]{:S(2)}, u32[]{:S(2)}) %collective-permute-start.15) | collective-permute-done | bytes 215072 | tf_op jit(solution)/shard_map/ppermute | solution.py:15
  184.7 1.2 copy.38
  (90 shorter events, 4.6 us)
Async XLA Ops:
  0.6 4.5 %copy-start.2 = (f32[512,560]{0,1:T(8,128)S(1)}, f32[512,560]{0,1:T(8,128)}, u32[]{:S(2)}) copy-start(f32[512,560]{0,1:T(8,128)} %param.7) | copy-start | bytes 3440644
  0.6 39.9 %collective-permute-start = (f32[512,560]{0,1:T(8,128)}, f32[512,560]{0,1:T(8,128)}, u32[]{:S(2)}, u32[]{:S(2)}) collective-permute-start(f32[512,560]{0,1:T(8,128)} %param.9), channel_id=1, source_target_pairs={{0,1},{1,0},{2,3},{3,2},{4,5},{5,4},{6,7},{7,6},{8,9},{9,8},{10,11... | collective-permute-start | bytes 3440648 | tf_op jit(solution)/shard_map/ppermute | solution.py:15
  1.2 30.1 %collective-permute-start.1 = (f32[512,560]{0,1:T(8,128)}, f32[512,560]{0,1:T(8,128)}, u32[]{:S(2)}, u32[]{:S(2)}) collective-permute-start(f32[512,560]{0,1:T(8,128)} %param.9), channel_id=1, source_target_pairs={{0,2},{1,3},{2,0},{3,1},{4,6},{5,7},{6,4},{7,5},{8,10},{9,11},{10,... | collective-permute-start | bytes 3440648 | tf_op jit(solution)/shard_map/ppermute | solution.py:15
  5.1 2.4 %copy-start.10 = (f32[512,560]{0,1:T(8,128)S(1)}, f32[512,560]{0,1:T(8,128)}, u32[]{:S(2)}) copy-start(f32[512,560]{0,1:T(8,128)} %param.5) | copy-start | bytes 3440644
  5.9 9.0 %collective-permute-start.3 = (f32[5,112,113]{2,1,0:T(8,128)S(1)}, f32[5,112,113]{2,1,0:T(8,128)S(1)}, u32[]{:S(2)}, u32[]{:S(2)}) collective-permute-start(f32[5,112,113]{2,1,0:T(8,128)S(1)} %fusion.7), channel_id=1, source_target_pairs={{0,4},{4,0},{8,12},{12,8},{16,20},{20,16},{24,28},{28,24},{1,5},{5... | collective-permute-start | bytes 759368 | tf_op jit(solution)/shard_map/ppermute | solution.py:15
  7.5 0.7 copy-start.13
  10.9 2.7 %copy-start.1 = (f32[5,512,512]{2,1,0:T(8,128)}, f32[5,512,512]{2,1,0:T(8,128)S(1)}, u32[]{:S(2)}) copy-start(f32[5,512,512]{2,1,0:T(8,128)S(1)} %broadcast_select_fusion.1) | copy-start | bytes 15728644
  10.9 5.6 %copy-start.9 = (f32[512,560]{0,1:T(8,128)S(1)}, f32[512,560]{0,1:T(8,128)}, u32[]{:S(2)}) copy-start(f32[512,560]{0,1:T(8,128)} %param.6) | copy-start | bytes 3440644
  14.8 9.1 %copy-start.20 = (f32[5,112,113]{2,1,0:T(8,128)}, f32[5,112,113]{2,1,0:T(8,128)S(1)}, u32[]{:S(2)}) copy-start(f32[5,112,113]{2,1,0:T(8,128)S(1)} %collective-permute-done.3) | copy-start | bytes 759364
  14.9 8.2 %collective-permute-start.4 = (f32[5,112,113]{2,1,0:T(8,128)S(1)}, f32[5,112,113]{2,1,0:T(8,128)S(1)}, u32[]{:S(2)}, u32[]{:S(2)}) collective-permute-start(f32[5,112,113]{2,1,0:T(8,128)S(1)} %add.132), channel_id=1, source_target_pairs={{0,8},{4,12},{8,0},{12,4},{16,24},{20,28},{24,16},{28,20},{1,9},{5... | collective-permute-start | bytes 759368 | tf_op jit(solution)/shard_map/ppermute | solution.py:15
  23.1 4.3 %copy-start.21 = (f32[5,112,113]{2,1,0:T(8,128)}, f32[5,112,113]{2,1,0:T(8,128)S(1)}, u32[]{:S(2)}) copy-start(f32[5,112,113]{2,1,0:T(8,128)S(1)} %collective-permute-done.4) | copy-start | bytes 759364
  23.9 14.7 %collective-permute-start.5 = (f32[5,112,113]{2,1,0:T(8,128)}, f32[5,112,113]{2,1,0:T(8,128)}, u32[]{:S(2)}, u32[]{:S(2)}) collective-permute-start(f32[5,112,113]{2,1,0:T(8,128)} %add.134), channel_id=1, source_target_pairs={{0,16},{4,20},{8,24},{12,28},{16,0},{20,4},{24,8},{28,12},{1,17},{... | collective-permute-start | bytes 759368 | tf_op jit(solution)/shard_map/ppermute | solution.py:15
  27.4 2.7 %copy-start.17 = (f32[512,560]{0,1:T(8,128)S(1)}, f32[512,560]{0,1:T(8,128)}, u32[]{:S(2)}) copy-start(f32[512,560]{0,1:T(8,128)} %param.9) | copy-start | bytes 3440644
  31.2 14.1 %collective-permute-start.2 = (f32[512,560]{0,1:T(8,128)}, f32[512,560]{0,1:T(8,128)S(1)}, u32[]{:S(2)}, u32[]{:S(2)}) collective-permute-start(f32[512,560]{0,1:T(8,128)} %collective-permute-done.1), channel_id=1, source_target_pairs={{0,1},{1,0},{2,3},{3,2},{4,5},{5,4},{6,7},{7,6},{8,9},{9,8},{10,11... | collective-permute-start | bytes 3440648 | tf_op jit(solution)/shard_map/ppermute | solution.py:15
  38.7 0.8 copy-start.11
  39.5 1.1 copy-start.5
  63.1 44.2 %collective-permute-start.7 = (f32[2,2,120,560]{2,3,1,0:T(8,128)}, f32[2,2,120,560]{2,3,1,0:T(8,128)}, u32[]{:S(2)}, u32[]{:S(2)}) collective-permute-start(f32[2,2,120,560]{2,3,1,0:T(8,128)} %bitcast.14), channel_id=1, source_target_pairs={{0,4},{4,0},{8,12},{12,8},{16,20},{20,16},{24,28},{28,24},{1,5},{5... | collective-permute-start | bytes 3225608 | tf_op jit(solution)/shard_map/ppermute | solution.py:15
  66.9 2.3 %copy-start.23 = (f32[2,2,64,560]{3,2,1,0:T(8,128)S(1)}, f32[2,2,64,560]{3,2,1,0:T(8,128)}, u32[]{:S(2)}) copy-start(f32[2,2,64,560]{3,2,1,0:T(8,128)} %dynamic-slice_bitcast_fusion.1) | copy-start | bytes 1720324
  69.2 15.4 %copy-start.8 = (f32[8,64,560]{2,1,0:T(8,128)S(1)}, f32[8,64,560]{2,1,0:T(8,128)}, u32[]{:S(2)}) copy-start(f32[8,64,560]{2,1,0:T(8,128)} %slice.27) | copy-start | bytes 3440644
  69.2 15.4 %collective-permute-start.6 = (f32[2,2,64,560]{3,2,1,0:T(8,128)S(1)}, f32[2,2,64,560]{3,2,1,0:T(8,128)S(1)}, u32[]{:S(2)}, u32[]{:S(2)}) collective-permute-start(f32[2,2,64,560]{3,2,1,0:T(8,128)S(1)} %copy-done.23), channel_id=1, source_target_pairs={{0,8},{4,12},{8,0},{12,4},{16,24},{20,28},{24,16},{28,20},{1,9},{5... | collective-permute-start | bytes 1720328 | tf_op jit(solution)/shard_map/ppermute | solution.py:15
  77.9 10.4 %copy-start.6 = (f32[5,512,113]{1,2,0:T(8,128)S(1)}, f32[5,512,113]{1,2,0:T(8,128)}, u32[]{:S(2)}) copy-start(f32[5,512,113]{1,2,0:T(8,128)} %copy-done.5) | copy-start | bytes 3471364
  84.7 17.7 %collective-permute-start.16 = (f32[2,64,560]{2,1,0:T(8,128)S(1)}, f32[2,64,560]{2,1,0:T(8,128)S(1)}, u32[]{:S(2)}, u32[]{:S(2)}) collective-permute-start(f32[2,64,560]{2,1,0:T(8,128)S(1)} %dynamic-slice_bitcast_fusion.4), channel_id=1, source_target_pairs={{0,16},{4,20},{8,24},{12,28},{16,0},{20,4},{24,8},{28,12},{1,17},{... | collective-permute-start | bytes 860168 | tf_op jit(solution)/shard_map/ppermute | solution.py:15
  88.3 1.3 copy-start.3
  88.3 1.3 copy-start.14
  94.6 1.4 copy-start.12
  105.0 10.1 %collective-permute-start.17 = (f32[64,560]{0,1:T(8,128)}, f32[64,560]{0,1:T(8,128)}, u32[]{:S(2)}, u32[]{:S(2)}) collective-permute-start(f32[64,560]{0,1:T(8,128)} %bitcast.122), channel_id=1, source_target_pairs={{0,4},{4,0},{8,12},{12,8},{16,20},{20,16},{24,28},{28,24},{1,5},{5... | collective-permute-start | bytes 430088 | tf_op jit(solution)/shard_map/ppermute | solution.py:15
  107.3 13.9 %collective-permute-start.8 = (f32[5,112,113]{2,1,0:T(8,128)}, f32[5,112,113]{2,1,0:T(8,128)S(1)}, u32[]{:S(2)}, u32[]{:S(2)}) collective-permute-start(f32[5,112,113]{2,1,0:T(8,128)} %fusion.11), channel_id=1, source_target_pairs={{0,4},{4,0},{8,12},{12,8},{16,20},{20,16},{24,28},{28,24},{1,5},{5... | collective-permute-start | bytes 759368 | tf_op jit(solution)/shard_map/ppermute | solution.py:15
  108.8 14.0 %copy-start = (f32[5,512,512]{2,1,0:T(8,128)S(1)}, f32[5,512,512]{2,1,0:T(8,128)}, u32[]{:S(2)}) copy-start(f32[5,512,512]{2,1,0:T(8,128)} %broadcast_select_fusion) | copy-start | bytes 15728644
  110.8 12.1 %copy-start.19 = (pred[512,560]{0,1:T(8,128)(4,1)S(1)}, pred[512,560]{0,1:T(8,128)(4,1)}, u32[]{:S(2)}) copy-start(pred[512,560]{0,1:T(8,128)(4,1)} %broadcast_compare_fusion.1) | copy-start | bytes 860164
  110.8 22.9 %collective-permute-start.11 = (f32[2,120,560]{1,2,0:T(8,128)S(1)}, f32[2,120,560]{1,2,0:T(8,128)S(1)}, u32[]{:S(2)}, u32[]{:S(2)}) collective-permute-start(f32[2,120,560]{1,2,0:T(8,128)S(1)} %dynamic-slice_bitcast_fusion.2), channel_id=1, source_target_pairs={{0,8},{4,12},{8,0},{12,4},{16,24},{20,28},{24,16},{28,20},{1,9},{5... | collective-permute-start | bytes 1612808 | tf_op jit(solution)/shard_map/ppermute | solution.py:15
  116.9 39.9 %collective-permute-start.13 = (f32[2,2,96,560]{3,2,1,0:T(8,128)}, f32[2,2,96,560]{3,2,1,0:T(8,128)S(1)}, u32[]{:S(2)}, u32[]{:S(2)}) collective-permute-start(f32[2,2,96,560]{3,2,1,0:T(8,128)} %dynamic-slice_bitcast_fusion), channel_id=1, source_target_pairs={{0,4},{4,0},{8,12},{12,8},{16,20},{20,16},{24,28},{28,24},{1,5},{5... | collective-permute-start | bytes 2580488 | tf_op jit(solution)/shard_map/ppermute | solution.py:15
  122.2 8.2 %collective-permute-start.9 = (f32[5,112,113]{2,1,0:T(8,128)S(1)}, f32[5,112,113]{2,1,0:T(8,128)S(1)}, u32[]{:S(2)}, u32[]{:S(2)}) collective-permute-start(f32[5,112,113]{2,1,0:T(8,128)S(1)} %add.142), channel_id=1, source_target_pairs={{0,8},{4,12},{8,0},{12,4},{16,24},{20,28},{24,16},{28,20},{1,9},{5... | collective-permute-start | bytes 759368 | tf_op jit(solution)/shard_map/ppermute | solution.py:15
  130.4 22.4 %collective-permute-start.10 = (f32[5,112,113]{2,1,0:T(8,128)S(1)}, f32[5,112,113]{2,1,0:T(8,128)S(1)}, u32[]{:S(2)}, u32[]{:S(2)}) collective-permute-start(f32[5,112,113]{2,1,0:T(8,128)S(1)} %add.144), channel_id=1, source_target_pairs={{0,16},{4,20},{8,24},{12,28},{16,0},{20,4},{24,8},{28,12},{1,17},{... | collective-permute-start | bytes 759368 | tf_op jit(solution)/shard_map/ppermute | solution.py:15
  133.8 19.1 %copy-start.15 = (f32[2,120,560]{1,2,0:T(8,128)}, f32[2,120,560]{1,2,0:T(8,128)S(1)}, u32[]{:S(2)}) copy-start(f32[2,120,560]{1,2,0:T(8,128)S(1)} %bitcast_add_fusion.3) | copy-start | bytes 1612804
  133.8 19.1 %copy-start.4 = (f32[512,560]{0,1:T(8,128)S(1)}, f32[512,560]{0,1:T(8,128)}, u32[]{:S(2)}) copy-start(f32[512,560]{0,1:T(8,128)} %param.7) | copy-start | bytes 3440644
  134.5 37.3 %collective-permute-start.12 = (f32[120,560]{0,1:T(8,128)}, f32[120,560]{0,1:T(8,128)}, u32[]{:S(2)}, u32[]{:S(2)}) collective-permute-start(f32[120,560]{0,1:T(8,128)} %dynamic-slice_bitcast_fusion.5), channel_id=1, source_target_pairs={{0,16},{4,20},{8,24},{12,28},{16,0},{20,4},{24,8},{28,12},{1,17},{... | collective-permute-start | bytes 806408 | tf_op jit(solution)/shard_map/ppermute | solution.py:15
  152.9 1.3 copy-start.18
  153.6 3.6 %slice-start = ((s8[5242880]{0:T(1024)(128)(4,1)}), s8[4194304]{0:T(1024)(128)(4,1)S(1)}, s32[]{:S(2)}) async-start(s8[5242880]{0:T(1024)(128)(4,1)} %bitcast.96), calls=%async_computation | async-start | bytes 8388608
  154.3 2.6 %copy-start.7 = (f32[8,96,560]{2,1,0:T(8,128)S(1)}, f32[8,96,560]{2,1,0:T(8,128)}, u32[]{:S(2)}) copy-start(f32[8,96,560]{2,1,0:T(8,128)} %slice.29) | copy-start | bytes 5160964
  154.3 2.9 %slice-start.1 = ((s8[5242880]{0:T(1024)(128)(4,1)}), s8[1048576]{0:T(1024)(128)(4,1)S(1)}, s32[]{:S(2)}) async-start(s8[5242880]{0:T(1024)(128)(4,1)} %bitcast.96), calls=%async_computation.1 | async-start | bytes 2097152
  157.0 11.4 %collective-permute-start.14 = (f32[2,96,560]{2,1,0:T(8,128)S(1)}, f32[2,96,560]{2,1,0:T(8,128)S(1)}, u32[]{:S(2)}, u32[]{:S(2)}) collective-permute-start(f32[2,96,560]{2,1,0:T(8,128)S(1)} %dynamic-slice_bitcast_fusion.3), channel_id=1, source_target_pairs={{0,8},{4,12},{8,0},{12,4},{16,24},{20,28},{24,16},{28,20},{1,9},{5... | collective-permute-start | bytes 1290248 | tf_op jit(solution)/shard_map/ppermute | solution.py:15
  159.7 12.2 %copy-start.16 = (f32[2,120,560]{1,2,0:T(8,128)S(1)}, f32[2,120,560]{1,2,0:T(8,128)}, u32[]{:S(2)}) copy-start(f32[2,120,560]{1,2,0:T(8,128)} %copy-done.15) | copy-start | bytes 1612804
  168.7 15.6 %copy-start.22 = (f32[64,560]{0,1:T(8,128)S(1)}, f32[64,560]{0,1:T(8,128)}, u32[]{:S(2)}) copy-start(f32[64,560]{0,1:T(8,128)} %bitcast_add_fusion.6) | copy-start | bytes 430084
  168.7 15.6 %collective-permute-start.15 = (f32[96,560]{0,1:T(8,128)S(1)}, f32[96,560]{0,1:T(8,128)S(1)}, u32[]{:S(2)}, u32[]{:S(2)}) collective-permute-start(f32[96,560]{0,1:T(8,128)S(1)} %bitcast.123), channel_id=1, source_target_pairs={{0,16},{4,20},{8,24},{12,28},{16,0},{20,4},{24,8},{28,12},{1,17},{... | collective-permute-start | bytes 645128 | tf_op jit(solution)/shard_map/ppermute | solution.py:15
